TPU v7x, 32 devices: a whole 2x2x4 slice. The times are simulated.
32 devices in a mesh: ent: 8 (over z, y), rel: 4 (over x, core).
Axes of the slice: x: 2, y: 2, z: 4, core: 2. Of those that a mesh axis runs over, the one named last changes fastest.
Arguments:
- entity_rows: bfloat16 [8192, 256], P('ent'), may hold values from -2.5 to 2.5
- request_rows: int32 [8, 8, 32], P('ent'), may hold values from 0 to 1023
- edge_heads: int32 [32768], P(('ent', 'rel')), may hold values from 0 to 1023
- edge_rels: int32 [32768], P(('ent', 'rel')), may hold values from 0 to 7
- edge_tails: int32 [32768], P(('ent', 'rel')), may hold values from 0 to 255
- edge_counts: int32 [32], P(('ent', 'rel')), may hold values from 1 to 1024, 20480 in all
- negative_rows: int32 [8192], P(('ent', 'rel')), may hold values from 0 to 1023
- relation_blocks: bfloat16 [32, 8, 32, 32], P('rel'), may hold values from -1 to 1
Outputs:
- entity_grad: float32 [8192, 256], P('ent')
- relation_grad: float32 [32, 8, 32, 32], P('rel')
Inputs may be any that keep to these rules, and one draw needn't show every extreme that they name: Edge slots of bucket b at or past edge_counts[b] are ignored; some bucket is full in every draw.
All inputs are finite; a program needn't handle non-finite values. No bound on the sum of `edge_counts` on one device may be relied on, other than what follows from the above.
Results may differ from a plain program's by a relative error of at most 0.009.
Values may be sent and summed in bfloat16 or wider, within the bound.
A program may use at most 64 MiB of HBM per device.

v0:
```python
import math

import jax
import jax.numpy as jnp
from jax import lax
from jax.sharding import PartitionSpec as P


def pick_rows(indices, source_table):
    row_total = indices.shape[0]
    block_size = math.gcd(row_total, 256)
    grouped = indices.reshape(row_total // block_size, block_size)
    columns = jnp.arange(source_table.shape[0], dtype=jnp.int32)

    def pick_block(index_block):
        one_hot = (index_block[:, None] == columns[None, :]).astype(jnp.bfloat16)
        return jnp.dot(one_hot, source_table, preferred_element_type=jnp.float32).astype(
            jnp.bfloat16
        )

    picked = lax.map(pick_block, grouped)
    return picked.reshape(row_total, source_table.shape[1])


def owner_add(indices, gradients, entity_count):
    start_value = jnp.zeros((entity_count, gradients.shape[1]), jnp.float32)
    return start_value.at[indices].add(gradients)


def local(
    entity_rows,
    request_rows,
    edge_heads,
    edge_rels,
    edge_tails,
    edge_counts,
    negative_rows,
    relation_blocks,
):
    entity_count, feature_width = entity_rows.shape
    part_count = request_rows.shape[1]
    slot_count = request_rows.shape[2]
    r_count, block_count, block_width = (
        relation_blocks.shape[0],
        relation_blocks.shape[1],
        relation_blocks.shape[2],
    )
    neg_count = negative_rows.shape[0]
    owner_lists = lax.all_to_all(request_rows, "ent", split_axis=1, concat_axis=0, tiled=True)
    wanted = pick_rows(owner_lists.reshape(-1), entity_rows).reshape(
        part_count, 1, slot_count, feature_width
    )
    fetched = lax.all_to_all(wanted, "ent", split_axis=0, concat_axis=1, tiled=True)
    fetched = fetched.reshape(part_count * slot_count, feature_width)
    neg_rows = pick_rows(negative_rows, entity_rows)
    edge_dev = edge_heads.shape[0]
    block_size = math.gcd(edge_dev, 256)
    block_total = edge_dev // block_size
    live_count = edge_counts[0]
    positions = jnp.arange(edge_dev, dtype=jnp.int32).reshape(block_total, block_size)
    entity_columns = jnp.arange(entity_count, dtype=jnp.int32)
    slot_columns = jnp.arange(part_count * slot_count, dtype=jnp.int32)
    rel_columns = jnp.arange(r_count, dtype=jnp.int32)
    contract_rows = (((0,), (0,)), ((), ()))

    def edge_block(running, block_inputs):
        slot_acc, entity_acc, neg_acc, relation_acc = running
        head_ids, rel_ids, tail_ids, places = block_inputs
        live_mask = (places < live_count).astype(jnp.float32)
        head_hot = (head_ids[:, None] == entity_columns[None, :]).astype(jnp.bfloat16)
        tail_hot = (tail_ids[:, None] == slot_columns[None, :]).astype(jnp.bfloat16)
        head_rows = jnp.dot(head_hot, entity_rows, preferred_element_type=jnp.float32).astype(
            jnp.bfloat16
        )
        tail_rows = jnp.dot(tail_hot, fetched, preferred_element_type=jnp.float32).astype(
            jnp.bfloat16
        )
        rel_hot = (rel_ids[:, None] == rel_columns[None, :]).astype(jnp.float32)
        head_split = head_rows.reshape(block_size, block_count, block_width)
        proj_all = jnp.einsum(
            "enb,rnbc->renc", head_split, relation_blocks, preferred_element_type=jnp.float32
        )
        projected = (
            jnp.sum(rel_hot.T[:, :, None, None] * proj_all, 0)
            .reshape(block_size, feature_width)
            .astype(jnp.bfloat16)
        )
        projected_wide = projected.astype(jnp.float32)
        positive = jnp.sum(projected_wide * tail_rows.astype(jnp.float32), -1)
        negative = lax.dot_general(
            projected, neg_rows, (((1,), (1,)), ((), ())), preferred_element_type=jnp.float32
        )
        pos_weight = -live_mask * jax.nn.sigmoid(-positive)
        neg_weight = (live_mask[:, None] * jax.nn.sigmoid(negative) / neg_count).astype(
            jnp.bfloat16
        )
        grad_proj = (
            pos_weight[:, None] * tail_rows.astype(jnp.float32)
            + jnp.dot(neg_weight, neg_rows, preferred_element_type=jnp.float32)
        ).astype(jnp.bfloat16)
        weighted = (pos_weight[:, None] * projected_wide).astype(jnp.bfloat16)
        grad_split = grad_proj.reshape(block_size, block_count, block_width)
        back_all = jnp.einsum(
            "enc,rnbc->renb", grad_split, relation_blocks, preferred_element_type=jnp.float32
        )
        head_grad = (
            jnp.sum(rel_hot.T[:, :, None, None] * back_all, 0)
            .reshape(block_size, feature_width)
            .astype(jnp.bfloat16)
        )
        slot_acc = slot_acc + lax.dot_general(
            tail_hot, weighted, contract_rows, preferred_element_type=jnp.float32
        )
        entity_acc = entity_acc + lax.dot_general(
            head_hot, head_grad, contract_rows, preferred_element_type=jnp.float32
        )
        neg_acc = neg_acc + lax.dot_general(
            neg_weight, projected, contract_rows, preferred_element_type=jnp.float32
        )
        masked_heads = rel_hot.T.astype(jnp.bfloat16)[:, :, None, None] * head_split[None]
        relation_acc = relation_acc + jnp.einsum(
            "renb,enc->rnbc", masked_heads, grad_split, preferred_element_type=jnp.float32
        )
        return ((slot_acc, entity_acc, neg_acc, relation_acc), None)

    start_values = (
        jnp.zeros((part_count * slot_count, feature_width), jnp.float32),
        jnp.zeros((entity_count, feature_width), jnp.float32),
        jnp.zeros((neg_count, feature_width), jnp.float32),
        jnp.zeros(relation_blocks.shape, jnp.float32),
    )
    block_inputs = (
        edge_heads.reshape(block_total, block_size),
        edge_rels.reshape(block_total, block_size),
        edge_tails.reshape(block_total, block_size),
        positions,
    )
    (slot_acc, entity_acc, neg_acc, relation_acc), _ = lax.scan(
        edge_block, start_values, block_inputs
    )
    neg_hot = (negative_rows[:, None] == entity_columns[None, :]).astype(jnp.bfloat16)
    entity_acc = entity_acc + lax.dot_general(
        neg_hot, neg_acc.astype(jnp.bfloat16), contract_rows, preferred_element_type=jnp.float32
    )
    slot_grads = slot_acc.reshape(1, part_count, slot_count, feature_width)
    returned = lax.all_to_all(
        slot_grads.astype(jnp.bfloat16), "ent", split_axis=1, concat_axis=0, tiled=True
    ).astype(slot_grads.dtype)
    entity_acc = entity_acc + owner_add(
        owner_lists.reshape(-1), returned.reshape(-1, feature_width), entity_count
    )
    entity_grad = lax.psum(entity_acc, "rel")
    relation_grad = lax.psum(relation_acc, "ent")
    return (entity_grad, relation_grad)


def solution(mesh):
    in_specs = (
        P("ent", None),
        P("ent", None, None),
        P(("ent", "rel")),
        P(("ent", "rel")),
        P(("ent", "rel")),
        P(("ent", "rel")),
        P(("ent", "rel")),
        P("rel", None, None, None),
    )
    out_specs = (P("ent", None), P("rel", None, None, None))
    return jax.shard_map(local, mesh=mesh, in_specs=in_specs, out_specs=out_specs, check_vma=False)
```

profile of v0, /device:TPU:0, one launch (start us, length us, event | category | flops | bytes accessed | tf_op | source)
XLA Modules:
  0.0 187.5 jit_solution(16742710074183567732)
XLA Ops:
  7.2 7.3 %all-to-all-start = ((s32[1,8,32]{2,0,1:T(1,128)}), s32[1,8,32]{2,0,1:T(1,128)S(1)}, u32[]{:S(2)}, u32[]{:S(2)}) async-start(s32[1,8,32]{2,0,1:T(1,128)} %bitcast.129), calls=%async_computation | async-start | bytes 8192 | tf_op jit(solution)/shard_map/all_to_all | solution.py:49
  14.5 1.5 convolution_convert_fusion.2
  16.0 4.9 %all-to-all-done = s32[1,8,32]{2,0,1:T(1,128)S(1)} async-done(((s32[1,8,32]{2,0,1:T(1,128)}), s32[1,8,32]{2,0,1:T(1,128)S(1)}, u32[]{:S(2)}, u32[]{:S(2)}) %all-to-all-start) | async-done | bytes 1056 | tf_op jit(solution)/shard_map/all_to_all | solution.py:49
  21.4 0.7 reduce.5
  22.1 2.1 %convolution_convert_fusion.3 = bf16[256,256]{1,0:T(8,128)(2,1)} fusion(bf16[1024,256]{1,0:T(8,128)(2,1)} %param.10, s32[256]{0:T(256)S(1)} %eq.102), kind=kOutput, calls=%fused_computation.51 | convolution fusion | flops 134545408 | bytes 656384 | tf_op jit(solution)/shard_map/while/body/eval_jaxpr/dot_general | solution.py:17
  24.2 3.4 %all-to-all-start.1 = ((bf16[8,1,32,256]{3,2,1,0:T(8,128)(2,1)}), bf16[8,1,32,256]{3,2,1,0:T(8,128)(2,1)S(1)}, u32[]{:S(2)}, u32[]{:S(2)}) async-start(bf16[8,1,32,256]{3,2,1,0:T(8,128)(2,1)} %bitcast.3), calls=%async_computation.1 | async-start | bytes 262144 | tf_op jit(solution)/shard_map/all_to_all | solution.py:53
  27.7 0.8 copy.24
  28.6 6.2 %all-to-all-done.1 = bf16[8,1,32,256]{3,2,1,0:T(8,128)(2,1)S(1)} async-done(((bf16[8,1,32,256]{3,2,1,0:T(8,128)(2,1)}), bf16[8,1,32,256]{3,2,1,0:T(8,128)(2,1)S(1)}, u32[]{:S(2)}, u32[]{:S(2)}) %all-to-all-start.1) | async-done | bytes 131104 | tf_op jit(solution)/shard_map/all_to_all | solution.py:53
  34.8 25.0 %while.3 = (s32[]{:T(128)}, f32[256,256]{1,0:T(8,128)S(1)}, f32[1024,256]{1,0:T(8,128)S(1)}, f32[256,256]{1,0:T(8,128)S(1)}, f32[8,8,32,32]{2,3,0,1:T(8,128)S(1)...) while((s32[]{:T(128)}, f32[256,256]{1,0:T(8,128)S(1)}, ...), condition=%wide.region_4.5_spmd.clone, body=%wide.region_0.4_spmd.clone.sunk | while | flops 544021760 | bytes 8048854 | solution.py:138
  34.8 0.7 compare_convert_fusion.2
  35.6 1.5 convolution_convert_fusion.5
  39.5 0.9 fusion.105
  40.5 0.6 convolution_add_fusion.9
  41.1 0.7 compare_convert_fusion.2
  41.9 1.5 convolution_convert_fusion.5
  45.8 0.9 fusion.105
  47.4 0.7 compare_convert_fusion.2
  48.1 1.5 convolution_convert_fusion.5
  52.1 0.9 fusion.105
  53.6 0.7 compare_convert_fusion.2
  54.4 1.5 convolution_convert_fusion.5
  58.3 0.9 fusion.105
  59.9 1.3 copy.25
  61.2 0.7 convert_element_type.109
  61.9 3.4 %all-to-all-start.2 = ((bf16[1,8,32,256]{3,2,0,1:T(8,128)(2,1)}), bf16[1,8,32,256]{3,2,0,1:T(8,128)(2,1)S(1)}, u32[]{:S(2)}, u32[]{:S(2)}) async-start(bf16[1,8,32,256]{3,2,0,1:T(8,128)(2,1)} %bitcast.6), calls=%async_computation.2 | async-start | bytes 262144 | tf_op jit(solution)/shard_map/all_to_all | solution.py:146
  65.9 8.7 %all-to-all-done.2 = bf16[1,8,32,256]{3,2,0,1:T(8,128)(2,1)S(1)} async-done(((bf16[1,8,32,256]{3,2,0,1:T(8,128)(2,1)}), bf16[1,8,32,256]{3,2,0,1:T(8,128)(2,1)S(1)}, u32[]{:S(2)}, u32[]{:S(2)}) %all-to-all-start.2) | async-done | bytes 131104 | tf_op jit(solution)/shard_map/all_to_all | solution.py:146
  74.6 2.4 %scatter_custom_fusion = f32[1024,256]{1,0:T(8,128)S(1)} fusion(f32[1024,256]{1,0:T(8,128)S(1)} %convolution_add_fusion.4, s32[256]{0:T(256)S(1)} %bitcast.130, bf16[256,256]{1,0:T(8,128)(2,1)S(1)} %bitcast.120), kind=kCustom, calls=%fused_computation.57 | custom fusion | flops 131072 | bytes 1179648 | tf_op jit(solution)/shard_map/scatter-add | solution.py:27
  77.0 1.0 copy-done
  77.9 60.7 %all-reduce.5.cloned.1.call-done = f32[8,8,32,32]{3,2,1,0:T(8,128)} async-done(((f32[8,8,32,32]{3,2,1,0:T(8,128)}), f32[8,8,32,32]{3,2,1,0:T(8,128)}) %all-reduce.5.cloned.1.call-update) | async-done | bytes 262160 | tf_op jit(solution)/shard_map/psum | solution.py:153
  138.6 38.8 %all-reduce.3.cloned.1.call-done = f32[1024,256]{1,0:T(8,128)} async-done(((f32[1024,256]{1,0:T(8,128)}), f32[1024,256]{1,0:T(8,128)}) %all-reduce.3.cloned.1.call-update) | async-done | bytes 1048592 | tf_op jit(solution)/shard_map/psum | solution.py:152
  177.4 2.3 %copy.47 = f32[1024,256]{1,0:T(8,128)} copy(f32[1024,256]{1,0:T(8,128)} %all-reduce.3.cloned.1.call-done) | data formatting | bytes 2097152
  179.7 1.0 copy.48
  (85 shorter events, 12.7 us)
Async XLA Ops:
  7.2 13.7 %all-to-all-start = ((s32[1,8,32]{2,0,1:T(1,128)}), s32[1,8,32]{2,0,1:T(1,128)S(1)}, u32[]{:S(2)}, u32[]{:S(2)}) async-start(s32[1,8,32]{2,0,1:T(1,128)} %bitcast.129), calls=%async_computation | async-start | bytes 8192 | tf_op jit(solution)/shard_map/all_to_all | solution.py:49
  14.5 13.2 %copy-start.4 = (s32[1024]{0:T(1024)S(1)}, s32[1024]{0:T(1024)}, u32[]{:S(2)}) copy-start(s32[1024]{0:T(1024)} %param.12) | copy-start | bytes 12292
  14.5 13.2 %copy-start.5 = (s32[1024]{0:T(1024)S(1)}, s32[1024]{0:T(1024)}, u32[]{:S(2)}) copy-start(s32[1024]{0:T(1024)} %param.13) | copy-start | bytes 12292
  14.5 13.2 %copy-start.6 = (s32[1024]{0:T(1024)S(1)}, s32[1024]{0:T(1024)}, u32[]{:S(2)}) copy-start(s32[1024]{0:T(1024)} %param.14) | copy-start | bytes 12292
  14.5 13.2 %copy-start.2 = (bf16[8,8,32,32]{3,2,1,0:T(8,128)(2,1)S(1)}, bf16[8,8,32,32]{3,2,1,0:T(8,128)(2,1)}, u32[]{:S(2)}) copy-start(bf16[8,8,32,32]{3,2,1,0:T(8,128)(2,1)} %param.17) | copy-start | bytes 393220
  24.2 10.7 %all-to-all-start.1 = ((bf16[8,1,32,256]{3,2,1,0:T(8,128)(2,1)}), bf16[8,1,32,256]{3,2,1,0:T(8,128)(2,1)S(1)}, u32[]{:S(2)}, u32[]{:S(2)}) async-start(bf16[8,1,32,256]{3,2,1,0:T(8,128)(2,1)} %bitcast.3), calls=%async_computation.1 | async-start | bytes 262144 | tf_op jit(solution)/shard_map/all_to_all | solution.py:53
  27.5 111.1 %all-reduce.5.cloned.1.call-start = ((), (), s32[]{:S(2)}) async-start(), calls=%async_computation.4 | async-start | bytes 2097152 | tf_op jit(solution)/shard_map/psum | solution.py:153
  34.8 2.3 %copy-start.3 = (bf16[8,8,32,32]{3,2,0,1:T(8,128)(2,1)S(1)}, bf16[8,8,32,32]{3,2,0,1:T(8,128)(2,1)}, u32[]{:S(2)}) copy-start(bf16[8,8,32,32]{3,2,0,1:T(8,128)(2,1)} %get-tuple-element.407) | copy-start | bytes 393220 | tf_op jit(solution)/shard_map/while
  41.1 2.3 %copy-start.3 = (bf16[8,8,32,32]{3,2,0,1:T(8,128)(2,1)S(1)}, bf16[8,8,32,32]{3,2,0,1:T(8,128)(2,1)}, u32[]{:S(2)}) copy-start(bf16[8,8,32,32]{3,2,0,1:T(8,128)(2,1)} %get-tuple-element.407) | copy-start | bytes 393220 | tf_op jit(solution)/shard_map/while
  47.3 2.3 %copy-start.3 = (bf16[8,8,32,32]{3,2,0,1:T(8,128)(2,1)S(1)}, bf16[8,8,32,32]{3,2,0,1:T(8,128)(2,1)}, u32[]{:S(2)}) copy-start(bf16[8,8,32,32]{3,2,0,1:T(8,128)(2,1)} %get-tuple-element.407) | copy-start | bytes 393220 | tf_op jit(solution)/shard_map/while
  53.6 2.3 %copy-start.3 = (bf16[8,8,32,32]{3,2,0,1:T(8,128)(2,1)S(1)}, bf16[8,8,32,32]{3,2,0,1:T(8,128)(2,1)}, u32[]{:S(2)}) copy-start(bf16[8,8,32,32]{3,2,0,1:T(8,128)(2,1)} %get-tuple-element.407) | copy-start | bytes 393220 | tf_op jit(solution)/shard_map/while
  61.2 4.1 %copy-start.7 = (s32[256]{0:T(256)S(1)}, s32[256]{0:T(256)}, u32[]{:S(2)}) copy-start(s32[256]{0:T(256)} %param.16) | copy-start | bytes 3076
  61.9 12.7 %all-to-all-start.2 = ((bf16[1,8,32,256]{3,2,0,1:T(8,128)(2,1)}), bf16[1,8,32,256]{3,2,0,1:T(8,128)(2,1)S(1)}, u32[]{:S(2)}, u32[]{:S(2)}) async-start(bf16[1,8,32,256]{3,2,0,1:T(8,128)(2,1)} %bitcast.6), calls=%async_computation.2 | async-start | bytes 262144 | tf_op jit(solution)/shard_map/all_to_all | solution.py:146
  65.3 112.1 %all-reduce.3.cloned.1.call-start = ((), (), s32[]{:S(2)}) async-start(), calls=%async_computation.3 | async-start | bytes 2097152 | tf_op jit(solution)/shard_map/psum | solution.py:152
  76.9 1.0 copy-start
  138.6 41.1 %copy-start.1 = (f32[8,8,32,32]{3,2,1,0:T(8,128)S(1)}, f32[8,8,32,32]{3,2,1,0:T(8,128)}, u32[]{:S(2)}) copy-start(f32[8,8,32,32]{3,2,1,0:T(8,128)} %all-reduce.5.cloned.1.call-done) | copy-start | bytes 786436
Sparse Core Ops, SparseCore 0:
  61.3 77.2 all-reduce.4
  141.7 35.6 all-reduce.2
where the time goes:
time: 188 us; the launch traced here: 187 us
  waiting for transfers between devices  119 us (63%)
  matrix products  25.6 us (14%)
  between operations  14.2 us (8%)
  starting transfers between devices  14.1 us (8%)
  local copies, waits for them, and re-layouts  7.17 us (4%)
  other arithmetic  6.62 us (4%)
    psum x1, waiting for transfers between devices, local(): relation_grad = lax.psum(relation_acc, 'ent')  60.7 us
    psum x1, waiting for transfers between devices, local(): entity_grad = lax.psum(entity_acc, 'rel')  38.8 us
    all_to_all x1, waiting for transfers between devices, local(): lax.all_to_all(slot_grads.astype(jnp.bfloat16), 'ent', split_axis=1, conc...  8.69 us
    all_to_all x1, starting transfers between devices, local(): lax.all_to_all(request_rows, 'ent', split_axis=1, concat_axis=0, tiled=True)  7.29 us
    all_to_all x1, waiting for transfers between devices, local(): lax.all_to_all(wanted, 'ent', split_axis=0, concat_axis=1, tiled=True)  6.18 us
    dot_general x4, matrix products, edge_block(): jnp.dot(head_hot, entity_rows, preferred_element_type=jnp.float32)  6.03 us
    unnamed x17, local copies, waits for them, and re-layouts  5.06 us
    all_to_all x1, waiting for transfers between devices, local(): lax.all_to_all(request_rows, 'ent', split_axis=1, concat_axis=0, tiled=True)  4.87 us
  transfers between devices with their start and end apart: 5, of which 5 were waited for; matrix products, arithmetic and copies ran while one was open for 3% of the time, Pallas kernels for 0%

commit v1 on v0

v1 whole, which is shorter than its diff:
```python
import functools

import jax
import jax.numpy as jnp
from jax import lax
from jax.experimental import pallas as pl
from jax.experimental.pallas import tpu as pltpu
from jax.sharding import PartitionSpec as P

MESH = pl.DeviceIdType.MESH
F32 = jnp.float32
BF16 = jnp.bfloat16
LANES = 128


def iota(shape, axis):
    return lax.broadcasted_iota(jnp.int32, shape, axis)


def hot(mask):
    return jnp.where(mask, 1.0, 0.0).astype(BF16)


def nn(a, b):
    return jnp.dot(a, b, preferred_element_type=F32)


def nt(a, b):
    return lax.dot_general(a, b, (((1,), (1,)), ((), ())), preferred_element_type=F32)


def tn(a, b):
    return lax.dot_general(a, b, (((0,), (0,)), ((), ())), preferred_element_type=F32)


def column(row):
    return jnp.transpose(jnp.broadcast_to(row, (LANES, LANES)))


def each(count, body):
    if count <= 8:
        for step in range(count):
            body(step)
    else:
        lax.fori_loop(0, count, lambda step, _: (body(step), 0)[1], 0)


def kernel(
    dims,
    counts_ref,
    entity_ref,
    request_ref,
    heads_ref,
    rels_ref,
    tails_ref,
    negs_ref,
    blocks_ref,
    sum_a_ref,
    sum_b_ref,
    rel_out_ref,
    request_wide,
    request_send,
    request_recv,
    want_send,
    fetched,
    slot_send,
    scatter_hot,
    grads,
    tail_hot_t,
    codes,
    hot_rows,
    operators,
    operators_t,
    masked_heads,
    masked_grads,
    projected,
    neg_weight,
    neg_rows,
    weighted,
    grad_proj,
    grad_proj_t,
    part_send,
    part_recv,
    own_half,
    rel_send,
    rel_recv,
    rel_own,
    request_sems,
    fetch_sems,
    slot_sems,
    part_sems,
    cross_sems,
    near_sems,
    far_sems,
    rs_sems,
    ag_sems,
):
    n_ent, n_rel = dims
    me, rel = lax.axis_index("ent"), lax.axis_index("rel")
    core, side = rel % 2, rel // 2
    near = side * 2 + (1 - core)
    cross = (1 - side) * 2 + core
    entities, width = entity_ref.shape
    slots = request_ref.shape[2]
    slot_total = n_ent * slots
    edges = heads_ref.shape[0] * LANES
    negs = negs_ref.shape[0] * LANES
    block = blocks_ref.shape[1]
    r_count = blocks_ref.shape[0] // width
    chunk = 256
    chunks = edges // chunk
    per = LANES // slots
    head_bits = (entities - 1).bit_length()
    rel_bits = (r_count - 1).bit_length()
    neg_at, slot_at = edges, edges + negs
    half = entities // 2
    live_count = counts_ref[0]

    barrier = pltpu.get_barrier_semaphore()

    def greet(step):
        pl.semaphore_signal(
            barrier, inc=1, device_id=(lax.rem(me + step + 1, n_ent), rel), device_id_type=MESH
        )

    each(n_ent - 1, greet)
    for partner in (near, cross):
        pl.semaphore_signal(barrier, inc=1, device_id=(me, partner), device_id_type=MESH)

    request_wide[...] = jnp.zeros_like(request_wide)
    request_wide[:, :slots] = request_ref[0]
    base = request_wide[...]
    wide = base
    for q in range(1, per):
        wide = wide + pltpu.roll(base, q * slots, 1)
    for p in range(n_ent):
        request_send[p] = jnp.broadcast_to(wide[p : p + 1], (8, LANES))
    request_recv[me] = request_send[me]

    pl.semaphore_wait(barrier, n_ent + 1)

    def exchange(src, dst, sems, step):
        target = lax.rem(me + step + 1, n_ent)
        return pltpu.make_async_remote_copy(
            src_ref=src.at[target],
            dst_ref=dst.at[me],
            send_sem=sems.at[0, target],
            recv_sem=sems.at[1, me],
            device_id=(target, rel),
            device_id_type=MESH,
        )

    def arrival(dst, sems, step):
        source = lax.rem(me + step + 1, n_ent)
        return pltpu.make_async_remote_copy(
            src_ref=dst.at[source],
            dst_ref=dst.at[source],
            send_sem=sems.at[0, source],
            recv_sem=sems.at[1, source],
            device_id=(source, rel),
            device_id_type=MESH,
        )

    def start_all(src, dst, sems):
        each(n_ent - 1, lambda step: exchange(src, dst, sems, step).start())

    def wait_all(dst, sems):
        each(n_ent - 1, lambda step: arrival(dst, sems, step).wait_recv())

    def drain_all(src, dst, sems):
        each(n_ent - 1, lambda step: exchange(src, dst, sems, step).wait_send())

    start_all(request_send, request_recv, request_sems)

    for k in range(edges // LANES):
        code = heads_ref[k : k + 1] + (
            (rels_ref[k : k + 1] + (tails_ref[k : k + 1] << rel_bits)) << head_bits
        )
        codes[k * LANES : (k + 1) * LANES] = column(code)
    lane = iota((LANES, LANES), 1)
    for k in range(negs // LANES):
        ids = column(negs_ref[k : k + 1])
        for c in range(entities // LANES):
            hot_rows[k * LANES : (k + 1) * LANES, c * LANES : (c + 1) * LANES] = hot(
                ids == lane + c * LANES
            )
    neg_rows[...] = nn(hot_rows[:negs], entity_ref[...]).astype(BF16)

    wait_all(request_recv, request_sems)
    request_rows = []
    lane8 = iota((8, LANES), 1) // slots
    for g in range(n_ent // per):
        row = request_recv[g * per]
        for q in range(1, per):
            row = jnp.where(lane8 == q, request_recv[g * per + q], row)
        row = row[:1]
        request_rows.append(row)
        ids = column(row)
        for c in range(entities // LANES):
            hot_rows[:LANES, c * LANES : (c + 1) * LANES] = hot(ids == lane + c * LANES)
        want_send[g * per : (g + 1) * per] = (
            nn(hot_rows[:LANES], entity_ref[...]).astype(BF16).reshape(per, slots, width)
        )
    fetched[me] = want_send[me]
    start_all(want_send, fetched, fetch_sems)

    spread = hot(iota((block, width), 1) % block == iota((block, width), 0))
    spread_t = hot(iota((width, block), 0) % block == iota((width, block), 1))
    diagonal = iota((width, width), 0) // block == iota((width, width), 1) // block
    for r in range(r_count):
        rows = slice(r * width, (r + 1) * width)
        one = blocks_ref[rows]
        operators[rows] = jnp.where(diagonal, nn(one, spread), 0.0).astype(BF16)
        operators_t[rows] = jnp.where(diagonal, nt(spread_t, one), 0.0).astype(BF16)

    def rel_masks(rows):
        ids = (codes[rows] >> head_bits) & (r_count - 1)
        return [hot(ids == r) for r in range(r_count)]

    def mask_by_rel(source, masks, target, rows):
        for r in range(r_count):
            for c in range(width // LANES):
                at = r * width + c * LANES
                target[rows, at : at + LANES] = source[:, c * LANES : (c + 1) * LANES] * masks[r]

    neg_grad = jnp.zeros((negs, width), F32)
    wide_lane = iota((chunk, LANES), 1)
    for i in range(chunks):
        rows = slice(i * chunk, (i + 1) * chunk)
        ids = codes[rows] & (entities - 1)
        for c in range(entities // LANES):
            hot_rows[:, c * LANES : (c + 1) * LANES] = hot(ids == wide_lane + c * LANES)
        head = nn(hot_rows[...], entity_ref[...]).astype(BF16)
        mask_by_rel(head, rel_masks(rows), masked_heads, rows)
        proj = nn(masked_heads[rows], operators[...]).astype(BF16)
        projected[rows] = proj
        score = nt(proj, neg_rows[...])
        live = iota((chunk, negs), 0) + i * chunk < live_count
        weight = jnp.where(live, jax.nn.sigmoid(score) * (1.0 / negs), 0.0).astype(BF16)
        neg_weight[rows] = weight
        neg_grad = neg_grad + tn(weight, proj)
    grads[neg_at : neg_at + negs] = neg_grad.astype(BF16)

    sub = iota((entities, LANES), 0)
    for k in range(edges // LANES):
        scatter_hot[:, k * LANES : (k + 1) * LANES] = hot(sub == heads_ref[k : k + 1])
    for k in range(negs // LANES):
        at = neg_at + k * LANES
        scatter_hot[:, at : at + LANES] = hot(sub == negs_ref[k : k + 1])
    for k, row in enumerate(request_rows):
        at = slot_at + k * LANES
        scatter_hot[:, at : at + LANES] = hot(sub == row)
    slot_sub = iota((slot_total, LANES), 0)
    for k in range(edges // LANES):
        tail_hot_t[:, k * LANES : (k + 1) * LANES] = hot(slot_sub == tails_ref[k : k + 1])

    wait_all(fetched, fetch_sems)
    table = fetched[...].reshape(slot_total, width)
    for i in range(chunks):
        rows = slice(i * chunk, (i + 1) * chunk)
        ids = codes[rows] >> (head_bits + rel_bits)
        tail_hot = jnp.concatenate(
            [hot(ids == wide_lane + c * LANES) for c in range(slot_total // LANES)], axis=1
        )
        tail = nn(tail_hot, table)
        proj = projected[rows].astype(F32)
        positive = jnp.sum(proj * tail, axis=1, keepdims=True)
        live = iota((chunk, 1), 0) + i * chunk < live_count
        pos_weight = jnp.where(live, -jax.nn.sigmoid(-positive), 0.0)
        weighted[rows] = (pos_weight * proj).astype(BF16)
        grad_proj[rows] = (pos_weight * tail + nn(neg_weight[rows], neg_rows[...])).astype(BF16)
    per_step = min(n_ent, 8)
    for g in range(n_ent // per_step):
        rows = slice(g * per_step * slots, (g + 1) * per_step * slots)
        slot_send[g * per_step : (g + 1) * per_step] = (
            nn(tail_hot_t[rows], weighted[...]).astype(BF16).reshape(per_step, slots, width)
        )
    slot_recv = grads.at[slot_at : slot_at + slot_total]

    def slot_copy(step):
        target = lax.rem(me + step + 1, n_ent)
        return pltpu.make_async_remote_copy(
            src_ref=slot_send.at[target],
            dst_ref=grads.at[pl.ds(pl.multiple_of(slot_at + me * slots, slots), slots)],
            send_sem=slot_sems.at[0, target],
            recv_sem=slot_sems.at[1, me],
            device_id=(target, rel),
            device_id_type=MESH,
        )

    def slot_arrival(step):
        source = lax.rem(me + step + 1, n_ent)
        return pltpu.make_async_remote_copy(
            src_ref=slot_send.at[source],
            dst_ref=grads.at[pl.ds(pl.multiple_of(slot_at + source * slots, slots), slots)],
            send_sem=slot_sems.at[0, source],
            recv_sem=slot_sems.at[1, source],
            device_id=(source, rel),
            device_id_type=MESH,
        )

    each(n_ent - 1, lambda step: slot_copy(step).start())
    grads[pl.ds(pl.multiple_of(slot_at + me * slots, slots), slots)] = slot_send[me]

    for i in range(chunks):
        rows = slice(i * chunk, (i + 1) * chunk)
        mask_by_rel(grad_proj[rows], rel_masks(rows), masked_grads, slice(0, chunk))
        grads[rows] = nn(masked_grads[...], operators_t[...]).astype(BF16)

    each(n_ent - 1, lambda step: slot_arrival(step).wait_recv())

    pieces = half // chunk
    part_copies = []
    for q in range(pieces):
        at = pl.multiple_of((1 - core) * half + q * chunk, chunk)
        part_send[q] = nn(scatter_hot[pl.ds(at, chunk)], grads[...]).astype(BF16)
        copy = pltpu.make_async_remote_copy(
            src_ref=part_send.at[q],
            dst_ref=part_recv.at[q],
            send_sem=part_sems.at[0, q],
            recv_sem=part_sems.at[1, q],
            device_id=(me, near),
            device_id_type=MESH,
        )
        copy.start()
        part_copies.append(copy)
    for q in range(pieces):
        at = pl.multiple_of(core * half + q * chunk, chunk)
        own_half[q] = nn(scatter_hot[pl.ds(at, chunk)], grads[...])
    cross_copies, near_copies = [], []
    for q in range(pieces):
        part_copies[q].wait_recv()
        sum_a_ref[core, q] = (own_half[q] + part_recv[q].astype(F32)).astype(BF16)
        copy = pltpu.make_async_remote_copy(
            src_ref=sum_a_ref.at[core, q],
            dst_ref=sum_b_ref.at[core, q],
            send_sem=cross_sems.at[0, q],
            recv_sem=cross_sems.at[1, q],
            device_id=(me, cross),
            device_id_type=MESH,
        )
        copy.start()
        cross_copies.append(copy)
        copy = pltpu.make_async_remote_copy(
            src_ref=sum_a_ref.at[core, q],
            dst_ref=sum_a_ref.at[core, q],
            send_sem=near_sems.at[0, q],
            recv_sem=near_sems.at[1, q],
            device_id=(me, near),
            device_id_type=MESH,
        )
        copy.start()
        near_copies.append(copy)

    wire = rel_send.dtype
    per_owner = rel_send.shape[1]
    grad_proj_t[...] = jnp.transpose(grad_proj[...])
    block_of_lane = iota((block, width), 1) // block
    step_rows = min(block, per_owner)
    for r in range(r_count):
        outer = nn(grad_proj_t[...], masked_heads[:, r * width : (r + 1) * width])
        small = jnp.zeros((block, width), F32)
        for n in range(width // block):
            small = small + jnp.where(
                block_of_lane == n, outer[n * block : (n + 1) * block], 0.0
            )
        for c in range(width // LANES):
            for t in range(block // step_rows):
                flat = (r * (width // LANES) + c) * block + t * step_rows
                owner, at = flat // per_owner, flat % per_owner
                rel_send[owner, at : at + step_rows] = small[
                    t * step_rows : (t + 1) * step_rows, c * LANES : (c + 1) * LANES
                ].astype(wire)
    start_all(rel_send, rel_recv, rs_sems)
    rel_recv[me] = rel_send[me]

    far_copies = []

    def forward(q):
        cross_copies[q].wait_recv()
        copy = pltpu.make_async_remote_copy(
            src_ref=sum_b_ref.at[core, q],
            dst_ref=sum_b_ref.at[core, q],
            send_sem=far_sems.at[0, q],
            recv_sem=far_sems.at[1, q],
            device_id=(me, near),
            device_id_type=MESH,
        )
        copy.start()
        far_copies.append(copy)

    for q in range(pieces - 1):
        forward(q)
    wait_all(rel_recv, rs_sems)
    total = rel_recv[0].astype(F32)
    for p in range(1, n_ent):
        total = total + rel_recv[p].astype(F32)
    rel_own[...] = total.astype(wire)
    rel_out_ref[me] = rel_own[...]

    def gather_copy(step):
        target = lax.rem(me + step + 1, n_ent)
        return pltpu.make_async_remote_copy(
            src_ref=rel_own,
            dst_ref=rel_out_ref.at[me],
            send_sem=ag_sems.at[0, target],
            recv_sem=ag_sems.at[1, me],
            device_id=(target, rel),
            device_id_type=MESH,
        )

    each(n_ent - 1, lambda step: gather_copy(step).start())
    forward(pieces - 1)

    wait_all(rel_out_ref, ag_sems)
    for copies in (near_copies, far_copies):
        for copy in copies:
            copy.wait_recv()
    drain_all(request_send, request_recv, request_sems)
    drain_all(want_send, fetched, fetch_sems)
    each(n_ent - 1, lambda step: slot_copy(step).wait_send())
    drain_all(rel_send, rel_recv, rs_sems)
    each(n_ent - 1, lambda step: gather_copy(step).wait_send())
    for copies in (part_copies, cross_copies, near_copies, far_copies):
        for copy in copies:
            copy.wait_send()


def local(
    n_ent,
    n_rel,
    entity_rows,
    request_rows,
    edge_heads,
    edge_rels,
    edge_tails,
    edge_counts,
    negative_rows,
    relation_blocks,
):
    entities, width = entity_rows.shape
    slots = request_rows.shape[2]
    slot_total = n_ent * slots
    edges = edge_heads.shape[0]
    negs = negative_rows.shape[0]
    r_count, block_count, block, _ = relation_blocks.shape
    chunk = 256
    pieces = entities // 2 // chunk
    stacked = r_count * width
    flat_rows = stacked * block // LANES
    per_owner = flat_rows // n_ent
    wire = BF16 if per_owner % 16 == 0 else F32
    terms = edges + negs + slot_total
    vmem = pltpu.VMEM
    dma = pltpu.SemaphoreType.DMA
    spec = pl.BlockSpec(memory_space=pltpu.VMEM)
    out_shape = (
        jax.ShapeDtypeStruct((2, pieces, chunk, width), BF16),
        jax.ShapeDtypeStruct((2, pieces, chunk, width), BF16),
        jax.ShapeDtypeStruct((n_ent, per_owner, LANES), wire),
    )
    scratch = [
        vmem((n_ent, LANES), jnp.int32),
        vmem((n_ent, 8, LANES), jnp.int32),
        vmem((n_ent, 8, LANES), jnp.int32),
        vmem((n_ent, slots, width), BF16),
        vmem((n_ent, slots, width), BF16),
        vmem((n_ent, slots, width), BF16),
        vmem((entities, terms), BF16),
        vmem((terms, width), BF16),
        vmem((slot_total, edges), BF16),
        vmem((edges, LANES), jnp.int32),
        vmem((chunk, entities), BF16),
        vmem((stacked, width), BF16),
        vmem((stacked, width), BF16),
        vmem((edges, stacked), BF16),
        vmem((chunk, stacked), BF16),
        vmem((edges, width), BF16),
        vmem((edges, negs), BF16),
        vmem((negs, width), BF16),
        vmem((edges, width), BF16),
        vmem((edges, width), BF16),
        vmem((width, edges), BF16),
        vmem((pieces, chunk, width), BF16),
        vmem((pieces, chunk, width), BF16),
        vmem((pieces, chunk, width), F32),
        vmem((n_ent, per_owner, LANES), wire),
        vmem((n_ent, per_owner, LANES), wire),
        vmem((per_owner, LANES), wire),
        dma((2, n_ent)),
        dma((2, n_ent)),
        dma((2, n_ent)),
        dma((2, pieces)),
        dma((2, pieces)),
        dma((2, pieces)),
        dma((2, pieces)),
        dma((2, n_ent)),
        dma((2, n_ent)),
    ]
    sum_a, sum_b, rel_flat = pl.pallas_call(
        functools.partial(kernel, (n_ent, n_rel)),
        out_shape=out_shape,
        in_specs=[pl.BlockSpec(memory_space=pltpu.SMEM)] + [spec] * 7,
        out_specs=(spec,) * 3,
        scratch_shapes=scratch,
        compiler_params=pltpu.CompilerParams(
            collective_id=0, has_side_effects=True, vmem_limit_bytes=56 * 1024 * 1024
        ),
    )(
        edge_counts,
        entity_rows,
        request_rows,
        edge_heads.reshape(edges // LANES, LANES),
        edge_rels.reshape(edges // LANES, LANES),
        edge_tails.reshape(edges // LANES, LANES),
        negative_rows.reshape(negs // LANES, LANES),
        relation_blocks.reshape(stacked, block),
    )
    entity_grad = (sum_a.astype(F32) + sum_b.astype(F32)).reshape(entities, width)
    relation_grad = (
        rel_flat.astype(F32)
        .reshape(stacked // LANES, block, LANES)
        .transpose(0, 2, 1)
        .reshape(relation_blocks.shape)
    )
    return entity_grad, relation_grad


def solution(mesh):
    in_specs = (
        P("ent", None),
        P("ent", None, None),
        P(("ent", "rel")),
        P(("ent", "rel")),
        P(("ent", "rel")),
        P(("ent", "rel")),
        P(("ent", "rel")),
        P("rel", None, None, None),
    )
    out_specs = (P("ent", None), P("rel", None, None, None))
    body = functools.partial(local, mesh.shape["ent"], mesh.shape["rel"])
    return jax.shard_map(body, mesh=mesh, in_specs=in_specs, out_specs=out_specs, check_vma=False)
```

time: 188 us -> 43.9 us (0.23)
  waiting for transfers between devices: 119 us -> 0 us
  Pallas kernels: 0 us -> 38.8 us
  matrix products: 25.6 us -> 0 us
  starting transfers between devices: 14.1 us -> 0 us
  between operations: 14.2 us -> 1.3 us
  local copies, waits for them, and re-layouts: 7.17 us -> 1.32 us
  other arithmetic: 6.62 us -> 2.34 us
    psum x2 -> x0, waiting for transfers between devices: 99.5 us -> none  [the longest x1 60.7 us: local(): relation_grad = lax.psum(relation_acc, 'ent')]
    pallas_call x0 -> x1, Pallas kernels: none -> 38.8 us  [local(): pl.pallas_call(functools.partial(kernel, (n_ent, n_rel)), out_shape=out_s...]
    dot_general x43 -> x0, matrix products: 25.6 us -> none  [the longest x4 6.03 us: edge_block(): jnp.dot(head_hot, entity_rows, preferred_element_type=jnp.float32)]
    all_to_all x3 -> x0, waiting for transfers between devices: 19.7 us -> none  [the longest x1 8.69 us: local(): lax.all_to_all(slot_grads.astype(jnp.bfloat16), 'ent', split_axis=1, conc...]
    all_to_all x3 -> x0, starting transfers between devices: 14.1 us -> none  [the longest x1 7.29 us: local(): lax.all_to_all(request_rows, 'ent', split_axis=1, concat_axis=0, tiled=True)]
    unnamed x17 -> x2, local copies, waits for them, and re-layouts: 5.06 us -> 0.01 us
    convert_element_type x9 -> x0, other arithmetic: 3.54 us -> none  [the longest x4 2.84 us: edge_block(): live_mask = (places < live_count).astype(jnp.float32)]
    scatter-add x1 -> x0, other arithmetic: 2.37 us -> none  [owner_add(): return start_value.at[indices].add(gradients)]
  transfers between devices with their start and end apart: 5 -> 0, of which waited for: 5 -> 0; matrix products, arithmetic and copies ran while one was open for 3% -> 0% of each run, Pallas kernels for 0% -> 0%
where the time goes in v1:
time: 43.9 us; the launch traced here: 43.8 us
  Pallas kernels  38.8 us (88%)
  other arithmetic  2.34 us (5%)
  local copies, waits for them, and re-layouts  1.32 us (3%)
  between operations  1.3 us (3%)
    pallas_call x1, Pallas kernels, local(): pl.pallas_call(functools.partial(kernel, (n_ent, n_rel)), out_shape=out_s...  38.8 us
    add x1, other arithmetic, local(): sum_a.astype(F32) + sum_b.astype(F32)  2.32 us
    reshape x1, local copies, waits for them, and re-layouts, local(): relation_grad = rel_flat.astype(F32).reshape(stacked // LANES, block, LAN...  1.31 us

profile of v1, /device:TPU:0, one launch (start us, length us, event | category | flops | bytes accessed | tf_op | source)
XLA Modules:
  0.0 43.8 jit_solution(1765674343850261161)
XLA Ops:
  1.3 38.8 %shard_map.95 = (bf16[2,2,256,256]{3,2,1,0:T(8,128)(2,1)}, bf16[2,2,256,256]{3,2,1,0:T(8,128)(2,1)}, bf16[8,64,128]{2,1,0:T(8,128)(2,1)}) custom-call(s32[1]{0:T(128)S(6)} %copy.11.counts_ref, bf16[1024,256]{1,0:T(8,128)(2,1)} %entity_ref.1, s32[1,8,32]{2,1,0:T(8,128)} %request_ref.1, s32[8,128]{1,0:T(8,128)} %bitcast.15, s32[8,128]{1,0:T(8,128)} %bitcast.16, ...), custom_call_target="tpu_custom_call" | custom-call | tf_op jit(solution)/shard_map/pallas_call | solution.py:500
  40.1 0.0 copy-start
  40.1 2.3 %convert_add_fusion = f32[2,2,256,256]{3,2,1,0:T(8,128)} fusion(bf16[2,2,256,256]{3,2,1,0:T(8,128)(2,1)} %get-tuple-element.6, bf16[2,2,256,256]{3,2,1,0:T(8,128)(2,1)} %get-tuple-element.5), kind=kLoop, calls=%fused_computation | loop fusion | flops 786432 | bytes 2097152 | tf_op jit(solution)/shard_map/add | solution.py:519
  42.4 0.0 copy-done
  42.5 1.3 %copy.10 = f32[16,128,32]{2,1,0:T(8,128)} copy(f32[16,128,32]{1,2,0:T(8,128)S(1)} %convert_bitcast_fusion) | data formatting | bytes 524288 | tf_op jit(solution)/shard_map/reshape | solution.py:524
  (1 shorter events, 0.0 us)
Async XLA Ops:
  40.1 2.3 %copy-start = (bf16[8,64,128]{2,1,0:T(8,128)(2,1)S(1)}, bf16[8,64,128]{2,1,0:T(8,128)(2,1)}, u32[]{:S(2)}) copy-start(bf16[8,64,128]{2,1,0:T(8,128)(2,1)} %get-tuple-element.7) | copy-start | bytes 393220

commit v2 on v1

--- a/solution.py
+++ b/solution.py
@@ -81,7 +81,6 @@
     grad_proj_t,
     part_send,
     part_recv,
-    own_half,
     rel_send,
     rel_recv,
     rel_own,
@@ -137,41 +136,6 @@
         request_send[p] = jnp.broadcast_to(wide[p : p + 1], (8, LANES))
     request_recv[me] = request_send[me]
 
-    pl.semaphore_wait(barrier, n_ent + 1)
-
-    def exchange(src, dst, sems, step):
-        target = lax.rem(me + step + 1, n_ent)
-        return pltpu.make_async_remote_copy(
-            src_ref=src.at[target],
-            dst_ref=dst.at[me],
-            send_sem=sems.at[0, target],
-            recv_sem=sems.at[1, me],
-            device_id=(target, rel),
-            device_id_type=MESH,
-        )
-
-    def arrival(dst, sems, step):
-        source = lax.rem(me + step + 1, n_ent)
-        return pltpu.make_async_remote_copy(
-            src_ref=dst.at[source],
-            dst_ref=dst.at[source],
-            send_sem=sems.at[0, source],
-            recv_sem=sems.at[1, source],
-            device_id=(source, rel),
-            device_id_type=MESH,
-        )
-
-    def start_all(src, dst, sems):
-        each(n_ent - 1, lambda step: exchange(src, dst, sems, step).start())
-
-    def wait_all(dst, sems):
-        each(n_ent - 1, lambda step: arrival(dst, sems, step).wait_recv())
-
-    def drain_all(src, dst, sems):
-        each(n_ent - 1, lambda step: exchange(src, dst, sems, step).wait_send())
-
-    start_all(request_send, request_recv, request_sems)
-
     for k in range(edges // LANES):
         code = heads_ref[k : k + 1] + (
             (rels_ref[k : k + 1] + (tails_ref[k : k + 1] << rel_bits)) << head_bits
@@ -185,6 +149,79 @@
                 ids == lane + c * LANES
             )
     neg_rows[...] = nn(hot_rows[:negs], entity_ref[...]).astype(BF16)
+
+    pl.semaphore_wait(barrier, n_ent + 1)
+
+    def exchange(src, dst, sems, step):
+        target = lax.rem(me + step + 1, n_ent)
+        return pltpu.make_async_remote_copy(
+            src_ref=src.at[target],
+            dst_ref=dst.at[me],
+            send_sem=sems.at[0, target],
+            recv_sem=sems.at[1, me],
+            device_id=(target, rel),
+            device_id_type=MESH,
+        )
+
+    def arrival(dst, sems, step):
+        source = lax.rem(me + step + 1, n_ent)
+        return pltpu.make_async_remote_copy(
+            src_ref=dst.at[source],
+            dst_ref=dst.at[source],
+            send_sem=sems.at[0, source],
+            recv_sem=sems.at[1, source],
+            device_id=(source, rel),
+            device_id_type=MESH,
+        )
+
+    def start_all(src, dst, sems):
+        each(n_ent - 1, lambda step: exchange(src, dst, sems, step).start())
+
+    def wait_all(dst, sems):
+        each(n_ent - 1, lambda step: arrival(dst, sems, step).wait_recv())
+
+    def drain_all(src, dst, sems):
+        each(n_ent - 1, lambda step: exchange(src, dst, sems, step).wait_send())
+
+    start_all(request_send, request_recv, request_sems)
+
+    spread = hot(iota((block, width), 1) % block == iota((block, width), 0))
+    spread_t = hot(iota((width, block), 0) % block == iota((width, block), 1))
+    diagonal = iota((width, width), 0) // block == iota((width, width), 1) // block
+    for r in range(r_count):
+        rows = slice(r * width, (r + 1) * width)
+        one = blocks_ref[rows]
+        operators[rows] = jnp.where(diagonal, nn(one, spread), 0.0).astype(BF16)
+        operators_t[rows] = jnp.where(diagonal, nt(spread_t, one), 0.0).astype(BF16)
+
+    def rel_masks(rows):
+        ids = (codes[rows] >> head_bits) & (r_count - 1)
+        return [hot(ids == r) for r in range(r_count)]
+
+    def mask_by_rel(source, masks, target, rows):
+        for r in range(r_count):
+            for c in range(width // LANES):
+                at = r * width + c * LANES
+                target[rows, at : at + LANES] = source[:, c * LANES : (c + 1) * LANES] * masks[r]
+
+    wide_lane = iota((chunk, LANES), 1)
+
+    def project(i):
+        rows = slice(i * chunk, (i + 1) * chunk)
+        ids = codes[rows] & (entities - 1)
+        for c in range(entities // LANES):
+            hot_rows[:, c * LANES : (c + 1) * LANES] = hot(ids == wide_lane + c * LANES)
+        head = nn(hot_rows[...], entity_ref[...]).astype(BF16)
+        mask_by_rel(head, rel_masks(rows), masked_heads, rows)
+        proj = nn(masked_heads[rows], operators[...]).astype(BF16)
+        projected[rows] = proj
+        score = nt(proj, neg_rows[...])
+        live = iota((chunk, negs), 0) + i * chunk < live_count
+        weight = jnp.where(live, jax.nn.sigmoid(score) * (1.0 / negs), 0.0).astype(BF16)
+        neg_weight[rows] = weight
+        return tn(weight, proj)
+
+    neg_grad = project(0)
 
     wait_all(request_recv, request_sems)
     request_rows = []
@@ -204,41 +241,8 @@
     fetched[me] = want_send[me]
     start_all(want_send, fetched, fetch_sems)
 
-    spread = hot(iota((block, width), 1) % block == iota((block, width), 0))
-    spread_t = hot(iota((width, block), 0) % block == iota((width, block), 1))
-    diagonal = iota((width, width), 0) // block == iota((width, width), 1) // block
-    for r in range(r_count):
-        rows = slice(r * width, (r + 1) * width)
-        one = blocks_ref[rows]
-        operators[rows] = jnp.where(diagonal, nn(one, spread), 0.0).astype(BF16)
-        operators_t[rows] = jnp.where(diagonal, nt(spread_t, one), 0.0).astype(BF16)
-
-    def rel_masks(rows):
-        ids = (codes[rows] >> head_bits) & (r_count - 1)
-        return [hot(ids == r) for r in range(r_count)]
-
-    def mask_by_rel(source, masks, target, rows):
-        for r in range(r_count):
-            for c in range(width // LANES):
-                at = r * width + c * LANES
-                target[rows, at : at + LANES] = source[:, c * LANES : (c + 1) * LANES] * masks[r]
-
-    neg_grad = jnp.zeros((negs, width), F32)
-    wide_lane = iota((chunk, LANES), 1)
-    for i in range(chunks):
-        rows = slice(i * chunk, (i + 1) * chunk)
-        ids = codes[rows] & (entities - 1)
-        for c in range(entities // LANES):
-            hot_rows[:, c * LANES : (c + 1) * LANES] = hot(ids == wide_lane + c * LANES)
-        head = nn(hot_rows[...], entity_ref[...]).astype(BF16)
-        mask_by_rel(head, rel_masks(rows), masked_heads, rows)
-        proj = nn(masked_heads[rows], operators[...]).astype(BF16)
-        projected[rows] = proj
-        score = nt(proj, neg_rows[...])
-        live = iota((chunk, negs), 0) + i * chunk < live_count
-        weight = jnp.where(live, jax.nn.sigmoid(score) * (1.0 / negs), 0.0).astype(BF16)
-        neg_weight[rows] = weight
-        neg_grad = neg_grad + tn(weight, proj)
+    for i in range(1, chunks):
+        neg_grad = neg_grad + project(i)
     grads[neg_at : neg_at + negs] = neg_grad.astype(BF16)
 
     sub = iota((entities, LANES), 0)
@@ -301,56 +305,6 @@
 
     each(n_ent - 1, lambda step: slot_copy(step).start())
     grads[pl.ds(pl.multiple_of(slot_at + me * slots, slots), slots)] = slot_send[me]
-
-    for i in range(chunks):
-        rows = slice(i * chunk, (i + 1) * chunk)
-        mask_by_rel(grad_proj[rows], rel_masks(rows), masked_grads, slice(0, chunk))
-        grads[rows] = nn(masked_grads[...], operators_t[...]).astype(BF16)
-
-    each(n_ent - 1, lambda step: slot_arrival(step).wait_recv())
-
-    pieces = half // chunk
-    part_copies = []
-    for q in range(pieces):
-        at = pl.multiple_of((1 - core) * half + q * chunk, chunk)
-        part_send[q] = nn(scatter_hot[pl.ds(at, chunk)], grads[...]).astype(BF16)
-        copy = pltpu.make_async_remote_copy(
-            src_ref=part_send.at[q],
-            dst_ref=part_recv.at[q],
-            send_sem=part_sems.at[0, q],
-            recv_sem=part_sems.at[1, q],
-            device_id=(me, near),
-            device_id_type=MESH,
-        )
-        copy.start()
-        part_copies.append(copy)
-    for q in range(pieces):
-        at = pl.multiple_of(core * half + q * chunk, chunk)
-        own_half[q] = nn(scatter_hot[pl.ds(at, chunk)], grads[...])
-    cross_copies, near_copies = [], []
-    for q in range(pieces):
-        part_copies[q].wait_recv()
-        sum_a_ref[core, q] = (own_half[q] + part_recv[q].astype(F32)).astype(BF16)
-        copy = pltpu.make_async_remote_copy(
-            src_ref=sum_a_ref.at[core, q],
-            dst_ref=sum_b_ref.at[core, q],
-            send_sem=cross_sems.at[0, q],
-            recv_sem=cross_sems.at[1, q],
-            device_id=(me, cross),
-            device_id_type=MESH,
-        )
-        copy.start()
-        cross_copies.append(copy)
-        copy = pltpu.make_async_remote_copy(
-            src_ref=sum_a_ref.at[core, q],
-            dst_ref=sum_a_ref.at[core, q],
-            send_sem=near_sems.at[0, q],
-            recv_sem=near_sems.at[1, q],
-            device_id=(me, near),
-            device_id_type=MESH,
-        )
-        copy.start()
-        near_copies.append(copy)
 
     wire = rel_send.dtype
     per_owner = rel_send.shape[1]
@@ -374,6 +328,55 @@
     start_all(rel_send, rel_recv, rs_sems)
     rel_recv[me] = rel_send[me]
 
+    for i in range(chunks):
+        rows = slice(i * chunk, (i + 1) * chunk)
+        mask_by_rel(grad_proj[rows], rel_masks(rows), masked_grads, slice(0, chunk))
+        grads[rows] = nn(masked_grads[...], operators_t[...]).astype(BF16)
+
+    each(n_ent - 1, lambda step: slot_arrival(step).wait_recv())
+
+    pieces = half // chunk
+    part_copies = []
+    for q in range(pieces):
+        at = pl.multiple_of((1 - core) * half + q * chunk, chunk)
+        part_send[q] = nn(scatter_hot[pl.ds(at, chunk)], grads[...]).astype(BF16)
+        copy = pltpu.make_async_remote_copy(
+            src_ref=part_send.at[q],
+            dst_ref=part_recv.at[q],
+            send_sem=part_sems.at[0, q],
+            recv_sem=part_sems.at[1, q],
+            device_id=(me, near),
+            device_id_type=MESH,
+        )
+        copy.start()
+        part_copies.append(copy)
+    cross_copies, near_copies = [], []
+    for q in range(pieces):
+        at = pl.multiple_of(core * half + q * chunk, chunk)
+        own = nn(scatter_hot[pl.ds(at, chunk)], grads[...])
+        part_copies[q].wait_recv()
+        sum_a_ref[core, q] = (own + part_recv[q].astype(F32)).astype(BF16)
+        copy = pltpu.make_async_remote_copy(
+            src_ref=sum_a_ref.at[core, q],
+            dst_ref=sum_b_ref.at[core, q],
+            send_sem=cross_sems.at[0, q],
+            recv_sem=cross_sems.at[1, q],
+            device_id=(me, cross),
+            device_id_type=MESH,
+        )
+        copy.start()
+        cross_copies.append(copy)
+        copy = pltpu.make_async_remote_copy(
+            src_ref=sum_a_ref.at[core, q],
+            dst_ref=sum_a_ref.at[core, q],
+            send_sem=near_sems.at[0, q],
+            recv_sem=near_sems.at[1, q],
+            device_id=(me, near),
+            device_id_type=MESH,
+        )
+        copy.start()
+        near_copies.append(copy)
+
     far_copies = []
 
     def forward(q):
@@ -389,8 +392,6 @@
         copy.start()
         far_copies.append(copy)
 
-    for q in range(pieces - 1):
-        forward(q)
     wait_all(rel_recv, rs_sems)
     total = rel_recv[0].astype(F32)
     for p in range(1, n_ent):
@@ -410,7 +411,8 @@
         )
 
     each(n_ent - 1, lambda step: gather_copy(step).start())
-    forward(pieces - 1)
+    for q in range(pieces):
+        forward(q)
 
     wait_all(rel_out_ref, ag_sems)
     for copies in (near_copies, far_copies):
@@ -424,6 +426,15 @@
     for copies in (part_copies, cross_copies, near_copies, far_copies):
         for copy in copies:
             copy.wait_send()
+
+
+def finish(a_ref, b_ref, rel_ref, entity_ref, relation_ref):
+    entity_ref[...] = a_ref[...].astype(F32) + b_ref[...].astype(F32)
+    block = relation_ref.shape[1]
+    for k in range(relation_ref.shape[0] // LANES):
+        relation_ref[k * LANES : (k + 1) * LANES] = jnp.transpose(
+            rel_ref[k * block : (k + 1) * block].astype(F32)
+        )
 
 
 def local(
@@ -483,7 +494,6 @@
         vmem((width, edges), BF16),
         vmem((pieces, chunk, width), BF16),
         vmem((pieces, chunk, width), BF16),
-        vmem((pieces, chunk, width), F32),
         vmem((n_ent, per_owner, LANES), wire),
         vmem((n_ent, per_owner, LANES), wire),
         vmem((per_owner, LANES), wire),
@@ -504,7 +514,7 @@
         out_specs=(spec,) * 3,
         scratch_shapes=scratch,
         compiler_params=pltpu.CompilerParams(
-            collective_id=0, has_side_effects=True, vmem_limit_bytes=56 * 1024 * 1024
+            collective_id=0, has_side_effects=True, vmem_limit_bytes=36 * 1024 * 1024
         ),
     )(
         edge_counts,
@@ -516,14 +526,24 @@
         negative_rows.reshape(negs // LANES, LANES),
         relation_blocks.reshape(stacked, block),
     )
-    entity_grad = (sum_a.astype(F32) + sum_b.astype(F32)).reshape(entities, width)
-    relation_grad = (
-        rel_flat.astype(F32)
-        .reshape(stacked // LANES, block, LANES)
-        .transpose(0, 2, 1)
-        .reshape(relation_blocks.shape)
+    steps = 4
+    tiles = stacked // LANES // steps
+    e_spec = pl.BlockSpec((entities // steps, width), lambda i: (i, 0))
+    entity_grad, relation_grad = pl.pallas_call(
+        finish,
+        grid=(steps,),
+        out_shape=(
+            jax.ShapeDtypeStruct((entities, width), F32),
+            jax.ShapeDtypeStruct((stacked, block), F32),
+        ),
+        in_specs=[e_spec, e_spec, pl.BlockSpec((tiles * block, LANES), lambda i: (i, 0))],
+        out_specs=(e_spec, pl.BlockSpec((tiles * LANES, block), lambda i: (i, 0))),
+    )(
+        sum_a.reshape(entities, width),
+        sum_b.reshape(entities, width),
+        rel_flat.reshape(flat_rows, LANES),
     )
-    return entity_grad, relation_grad
+    return entity_grad, relation_grad.reshape(relation_blocks.shape)
 
 
 def solution(mesh):

time: 43.9 us -> 45.6 us (1.039)
  local copies, waits for them, and re-layouts: 1.32 us -> 6.34 us
  other arithmetic: 2.34 us -> 0 us
  Pallas kernels: 38.8 us -> 37.6 us
    unnamed x2 -> x20, local copies, waits for them, and re-layouts: 0.01 us -> 6.34 us
    pallas_call x1, Pallas kernels: 38.8 us -> 34 us  [local(): pl.pallas_call(functools.partial(kernel, (n_ent, n_rel)), out_shape=out_s...]
    pallas_call x0 -> x1, Pallas kernels: none -> 3.62 us  [local(): pl.pallas_call(finish, grid=(steps,), out_shape=(jax.ShapeDtypeStruct((en...]
    add x1 -> x0, other arithmetic: 2.32 us -> none  [local(): sum_a.astype(F32) + sum_b.astype(F32)]
    reshape x1 -> x0, local copies, waits for them, and re-layouts: 1.31 us -> none  [local(): relation_grad = rel_flat.astype(F32).reshape(stacked // LANES, block, LAN...]
where the time goes in v2:
time: 45.6 us; the launch traced here: 45.2 us
  Pallas kernels  37.6 us (82%)
  local copies, waits for them, and re-layouts  6.34 us (14%)
  between operations  1.33 us (3%)
    pallas_call x1, Pallas kernels, local(): pl.pallas_call(functools.partial(kernel, (n_ent, n_rel)), out_shape=out_s...  34 us
    unnamed x20, local copies, waits for them, and re-layouts  6.34 us
    pallas_call x1, Pallas kernels, local(): pl.pallas_call(finish, grid=(steps,), out_shape=(jax.ShapeDtypeStruct((en...  3.62 us

profile of v2, /device:TPU:0, one launch (start us, length us, event | category | flops | bytes accessed | tf_op | source)
XLA Modules:
  0.0 45.2 jit_solution(9662864846295036091)
XLA Ops:
  1.3 0.0 copy-start.6
  1.3 0.0 copy-start.5
  1.3 0.0 copy-start.9
  1.3 0.7 %copy-done.6 = s32[1024]{0:T(1024)S(1)} copy-done((s32[1024]{0:T(1024)S(1)}, s32[1024]{0:T(1024)}, u32[]{:S(2)}) %copy-start.6) | copy-done | bytes 4120
  2.0 0.0 copy-done.5
  2.0 0.0 copy-done.9
  2.0 0.0 copy-start
  2.0 1.0 %copy-done = bf16[1024,256]{1,0:T(8,128)(2,1)S(1)} copy-done((bf16[1024,256]{1,0:T(8,128)(2,1)S(1)}, bf16[1024,256]{1,0:T(8,128)(2,1)}, u32[]{:S(2)}) %copy-start) | copy-done | bytes 524312
  3.0 0.0 copy-start.1
  3.0 1.0 %copy-done.1 = bf16[8,8,32,32]{3,2,1,0:T(8,128)(2,1)S(1)} copy-done((bf16[8,8,32,32]{3,2,1,0:T(8,128)(2,1)S(1)}, bf16[8,8,32,32]{3,2,1,0:T(8,128)(2,1)}, u32[]{:S(2)}) %copy-start.1) | copy-done | bytes 131096
  4.1 0.0 copy-start.7
  4.1 0.7 %copy-done.7 = s32[1024]{0:T(1024)S(1)} copy-done((s32[1024]{0:T(1024)S(1)}, s32[1024]{0:T(1024)}, u32[]{:S(2)}) %copy-start.7) | copy-done | bytes 4120
  4.8 0.0 copy-start.8
  4.8 0.7 %copy-done.8 = s32[1024]{0:T(1024)S(1)} copy-done((s32[1024]{0:T(1024)S(1)}, s32[1024]{0:T(1024)}, u32[]{:S(2)}) %copy-start.8) | copy-done | bytes 4120
  5.4 34.0 %shard_map.95 = (bf16[2,2,256,256]{3,2,1,0:T(8,128)(2,1)S(1)}, bf16[2,2,256,256]{3,2,1,0:T(8,128)(2,1)S(1)}, bf16[8,64,128]{2,1,0:T(8,128)(2,1)S(1)}) custom-call(s32[1]{0:T(128)S(6)} %copy.10.counts_ref, bf16[1024,256]{1,0:T(8,128)(2,1)S(1)} %copy-done, s32[1,8,32]{2,1,0:T(8,128)S(1)} %copy-done.5, s32[8,128]{1,0:T(8,128)S(1)} %bitcast.13, ...), custom_call_target="tpu_custom_call" | custom-call | tf_op jit(solution)/shard_map/pallas_call | solution.py:510
  39.4 0.0 copy-start.2
  39.4 0.8 %copy-done.2 = bf16[2,2,256,256]{3,2,1,0:T(8,128)(2,1)} copy-done((bf16[2,2,256,256]{3,2,1,0:T(8,128)(2,1)}, bf16[2,2,256,256]{3,2,1,0:T(8,128)(2,1)S(1)}, u32[]{:S(2)}) %copy-start.2) | copy-done | bytes 524312
  40.2 0.0 copy-start.3
  40.2 0.8 %copy-done.3 = bf16[2,2,256,256]{3,2,1,0:T(8,128)(2,1)} copy-done((bf16[2,2,256,256]{3,2,1,0:T(8,128)(2,1)}, bf16[2,2,256,256]{3,2,1,0:T(8,128)(2,1)S(1)}, u32[]{:S(2)}) %copy-start.3) | copy-done | bytes 524312
  41.0 0.0 copy-start.4
  41.0 0.6 %copy-done.4 = bf16[8,64,128]{2,1,0:T(8,128)(2,1)} copy-done((bf16[8,64,128]{2,1,0:T(8,128)(2,1)}, bf16[8,64,128]{2,1,0:T(8,128)(2,1)S(1)}, u32[]{:S(2)}) %copy-start.4) | copy-done | bytes 131096
  41.6 3.6 %shard_map.96 = (f32[1024,256]{1,0:T(8,128)}, f32[2048,32]{1,0:T(8,128)}) custom-call(bf16[1024,256]{1,0:T(8,128)(2,1)} %bitcast.10, bf16[1024,256]{1,0:T(8,128)(2,1)} %bitcast.11, bf16[512,128]{1,0:T(8,128)(2,1)} %bitcast.12), custom_call_target="tpu_custom_call" | custom-call | tf_op jit(solution)/shard_map/pallas_call | solution.py:532
Async XLA Ops:
  1.3 0.7 %copy-start.6 = (s32[1024]{0:T(1024)S(1)}, s32[1024]{0:T(1024)}, u32[]{:S(2)}) copy-start(s32[1024]{0:T(1024)} %param.10) | copy-start | bytes 12292
  1.3 0.7 %copy-start.5 = (s32[1,8,32]{2,1,0:T(8,128)S(1)}, s32[1,8,32]{2,1,0:T(8,128)}, u32[]{:S(2)}) copy-start(s32[1,8,32]{2,1,0:T(8,128)} %request_ref.1) | copy-start | bytes 3076
  1.3 0.7 %copy-start.9 = (s32[256]{0:T(256)S(1)}, s32[256]{0:T(256)}, u32[]{:S(2)}) copy-start(s32[256]{0:T(256)} %param.14) | copy-start | bytes 3076
  2.0 1.0 %copy-start = (bf16[1024,256]{1,0:T(8,128)(2,1)S(1)}, bf16[1024,256]{1,0:T(8,128)(2,1)}, u32[]{:S(2)}) copy-start(bf16[1024,256]{1,0:T(8,128)(2,1)} %entity_ref.1) | copy-start | bytes 1572868
  3.0 1.0 %copy-start.1 = (bf16[8,8,32,32]{3,2,1,0:T(8,128)(2,1)S(1)}, bf16[8,8,32,32]{3,2,1,0:T(8,128)(2,1)}, u32[]{:S(2)}) copy-start(bf16[8,8,32,32]{3,2,1,0:T(8,128)(2,1)} %param.15) | copy-start | bytes 393220
  4.1 0.7 %copy-start.7 = (s32[1024]{0:T(1024)S(1)}, s32[1024]{0:T(1024)}, u32[]{:S(2)}) copy-start(s32[1024]{0:T(1024)} %param.11) | copy-start | bytes 12292
  4.8 0.7 %copy-start.8 = (s32[1024]{0:T(1024)S(1)}, s32[1024]{0:T(1024)}, u32[]{:S(2)}) copy-start(s32[1024]{0:T(1024)} %param.12) | copy-start | bytes 12292
  39.4 0.8 %copy-start.2 = (bf16[2,2,256,256]{3,2,1,0:T(8,128)(2,1)}, bf16[2,2,256,256]{3,2,1,0:T(8,128)(2,1)S(1)}, u32[]{:S(2)}) copy-start(bf16[2,2,256,256]{3,2,1,0:T(8,128)(2,1)S(1)} %get-tuple-element.7) | copy-start | bytes 1572868
  40.2 0.8 %copy-start.3 = (bf16[2,2,256,256]{3,2,1,0:T(8,128)(2,1)}, bf16[2,2,256,256]{3,2,1,0:T(8,128)(2,1)S(1)}, u32[]{:S(2)}) copy-start(bf16[2,2,256,256]{3,2,1,0:T(8,128)(2,1)S(1)} %get-tuple-element.8) | copy-start | bytes 1572868
  41.0 0.6 %copy-start.4 = (bf16[8,64,128]{2,1,0:T(8,128)(2,1)}, bf16[8,64,128]{2,1,0:T(8,128)(2,1)S(1)}, u32[]{:S(2)}) copy-start(bf16[8,64,128]{2,1,0:T(8,128)(2,1)S(1)} %get-tuple-element.9) | copy-start | bytes 393220

commit v3 on v2

--- a/solution.py
+++ b/solution.py
@@ -47,6 +47,16 @@
 
 def kernel(
     dims,
+    counts_hbm,
+    entity_hbm,
+    request_hbm,
+    heads_hbm,
+    rels_hbm,
+    tails_hbm,
+    negs_hbm,
+    blocks_hbm,
+    entity_out,
+    relation_out,
     counts_ref,
     entity_ref,
     request_ref,
@@ -58,6 +68,8 @@
     sum_a_ref,
     sum_b_ref,
     rel_out_ref,
+    entity_stage,
+    relation_stage,
     request_wide,
     request_send,
     request_recv,
@@ -93,6 +105,9 @@
     far_sems,
     rs_sems,
     ag_sems,
+    in_sems,
+    entity_sems,
+    relation_sems,
 ):
     n_ent, n_rel = dims
     me, rel = lax.axis_index("ent"), lax.axis_index("rel")
@@ -106,14 +121,32 @@
     negs = negs_ref.shape[0] * LANES
     block = blocks_ref.shape[1]
     r_count = blocks_ref.shape[0] // width
-    chunk = 256
+    chunk = masked_grads.shape[0]
     chunks = edges // chunk
+    piece = sum_a_ref.shape[2]
     per = LANES // slots
     head_bits = (entities - 1).bit_length()
     rel_bits = (r_count - 1).bit_length()
     neg_at, slot_at = edges, edges + negs
     half = entities // 2
-    live_count = counts_ref[0]
+
+    loads = [
+        pltpu.make_async_copy(src, dst, in_sems.at[k])
+        for k, (src, dst) in enumerate(
+            (
+                (request_hbm, request_ref),
+                (heads_hbm, heads_ref),
+                (rels_hbm, rels_ref),
+                (tails_hbm, tails_ref),
+                (negs_hbm, negs_ref),
+                (entity_hbm, entity_ref),
+                (blocks_hbm, blocks_ref),
+                (counts_hbm, counts_ref),
+            )
+        )
+    ]
+    for load in loads:
+        load.start()
 
     barrier = pltpu.get_barrier_semaphore()
 
@@ -127,6 +160,7 @@
         pl.semaphore_signal(barrier, inc=1, device_id=(me, partner), device_id_type=MESH)
 
     request_wide[...] = jnp.zeros_like(request_wide)
+    loads[0].wait()
     request_wide[:, :slots] = request_ref[0]
     base = request_wide[...]
     wide = base
@@ -136,6 +170,8 @@
         request_send[p] = jnp.broadcast_to(wide[p : p + 1], (8, LANES))
     request_recv[me] = request_send[me]
 
+    for load in loads[1:5]:
+        load.wait()
     for k in range(edges // LANES):
         code = heads_ref[k : k + 1] + (
             (rels_ref[k : k + 1] + (tails_ref[k : k + 1] << rel_bits)) << head_bits
@@ -148,6 +184,7 @@
             hot_rows[k * LANES : (k + 1) * LANES, c * LANES : (c + 1) * LANES] = hot(
                 ids == lane + c * LANES
             )
+    loads[5].wait()
     neg_rows[...] = nn(hot_rows[:negs], entity_ref[...]).astype(BF16)
 
     pl.semaphore_wait(barrier, n_ent + 1)
@@ -188,6 +225,9 @@
     spread = hot(iota((block, width), 1) % block == iota((block, width), 0))
     spread_t = hot(iota((width, block), 0) % block == iota((width, block), 1))
     diagonal = iota((width, width), 0) // block == iota((width, width), 1) // block
+    loads[6].wait()
+    loads[7].wait()
+    live_count = counts_ref[0]
     for r in range(r_count):
         rows = slice(r * width, (r + 1) * width)
         one = blocks_ref[rows]
@@ -335,62 +375,47 @@
 
     each(n_ent - 1, lambda step: slot_arrival(step).wait_recv())
 
-    pieces = half // chunk
-    part_copies = []
-    for q in range(pieces):
-        at = pl.multiple_of((1 - core) * half + q * chunk, chunk)
-        part_send[q] = nn(scatter_hot[pl.ds(at, chunk)], grads[...]).astype(BF16)
+    pieces = half // piece
+    pair = 2
+    part_copies, cross_copies, near_copies, far_copies = [], [], [], []
+
+    def near_copy(src, dst, sems, q, target):
         copy = pltpu.make_async_remote_copy(
-            src_ref=part_send.at[q],
-            dst_ref=part_recv.at[q],
-            send_sem=part_sems.at[0, q],
-            recv_sem=part_sems.at[1, q],
-            device_id=(me, near),
+            src_ref=src,
+            dst_ref=dst,
+            send_sem=sems.at[0, q],
+            recv_sem=sems.at[1, q],
+            device_id=(me, target),
             device_id_type=MESH,
         )
         copy.start()
-        part_copies.append(copy)
-    cross_copies, near_copies = [], []
-    for q in range(pieces):
-        at = pl.multiple_of(core * half + q * chunk, chunk)
-        own = nn(scatter_hot[pl.ds(at, chunk)], grads[...])
-        part_copies[q].wait_recv()
-        sum_a_ref[core, q] = (own + part_recv[q].astype(F32)).astype(BF16)
-        copy = pltpu.make_async_remote_copy(
-            src_ref=sum_a_ref.at[core, q],
-            dst_ref=sum_b_ref.at[core, q],
-            send_sem=cross_sems.at[0, q],
-            recv_sem=cross_sems.at[1, q],
-            device_id=(me, cross),
-            device_id_type=MESH,
+        return copy
+
+    for g in range(pieces // pair):
+        at = pl.multiple_of((1 - core) * half + g * pair * piece, pair * piece)
+        part = nn(scatter_hot[pl.ds(at, pair * piece)], grads[...]).astype(BF16)
+        for q in range(g * pair, (g + 1) * pair):
+            low = (q - g * pair) * piece
+            part_send[q] = part[low : low + piece]
+            part_copies.append(near_copy(part_send.at[q], part_recv.at[q], part_sems, q, near))
+    for g in range(pieces // pair):
+        at = pl.multiple_of(core * half + g * pair * piece, pair * piece)
+        own = nn(scatter_hot[pl.ds(at, pair * piece)], grads[...])
+        for q in range(g * pair, (g + 1) * pair):
+            low = (q - g * pair) * piece
+            part_copies[q].wait_recv()
+            sum_a_ref[core, q] = (own[low : low + piece] + part_recv[q].astype(F32)).astype(BF16)
+            mine = sum_a_ref.at[core, q]
+            cross_copies.append(near_copy(mine, sum_b_ref.at[core, q], cross_sems, q, cross))
+            near_copies.append(near_copy(mine, mine, near_sems, q, near))
+
+    def write_entity(which, q):
+        entity_stage[which, q] = sum_a_ref[which, q].astype(F32) + sum_b_ref[which, q].astype(F32)
+        copy = pltpu.make_async_copy(
+            entity_stage.at[which, q], entity_out.at[which, q], entity_sems.at[which, q]
         )
         copy.start()
-        cross_copies.append(copy)
-        copy = pltpu.make_async_remote_copy(
-            src_ref=sum_a_ref.at[core, q],
-            dst_ref=sum_a_ref.at[core, q],
-            send_sem=near_sems.at[0, q],
-            recv_sem=near_sems.at[1, q],
-            device_id=(me, near),
-            device_id_type=MESH,
-        )
-        copy.start()
-        near_copies.append(copy)
-
-    far_copies = []
-
-    def forward(q):
-        cross_copies[q].wait_recv()
-        copy = pltpu.make_async_remote_copy(
-            src_ref=sum_b_ref.at[core, q],
-            dst_ref=sum_b_ref.at[core, q],
-            send_sem=far_sems.at[0, q],
-            recv_sem=far_sems.at[1, q],
-            device_id=(me, near),
-            device_id_type=MESH,
-        )
-        copy.start()
-        far_copies.append(copy)
+        return copy
 
     wait_all(rel_recv, rs_sems)
     total = rel_recv[0].astype(F32)
@@ -411,13 +436,43 @@
         )
 
     each(n_ent - 1, lambda step: gather_copy(step).start())
-    for q in range(pieces):
+    stores = []
+
+    def forward(q):
+        cross_copies[q].wait_recv()
+        theirs = sum_b_ref.at[core, q]
+        far_copies.append(near_copy(theirs, theirs, far_sems, q, near))
+        stores.append(write_entity(core, q))
+
+    def finish_other(q):
+        near_copies[q].wait_recv()
+        far_copies[q].wait_recv()
+        stores.append(write_entity(1 - core, q))
+
+    for q in range(pieces - 1):
         forward(q)
-
     wait_all(rel_out_ref, ag_sems)
-    for copies in (near_copies, far_copies):
-        for copy in copies:
-            copy.wait_recv()
+    for k in range(relation_stage.shape[0] // LANES):
+        parts = []
+        for t in range(block // step_rows):
+            owner, at = divmod(k * block + t * step_rows, per_owner)
+            parts.append(rel_out_ref[owner, at : at + step_rows].astype(F32))
+        tile = parts[0] if len(parts) == 1 else jnp.concatenate(parts, axis=0)
+        relation_stage[k * LANES : (k + 1) * LANES] = jnp.transpose(tile)
+    store_rows = relation_stage.shape[0] // relation_sems.shape[0]
+    for k in range(relation_sems.shape[0]):
+        rows = pl.ds(k * store_rows, store_rows)
+        copy = pltpu.make_async_copy(
+            relation_stage.at[rows], relation_out.at[rows], relation_sems.at[k]
+        )
+        copy.start()
+        stores.append(copy)
+    for q in range(pieces - 1):
+        finish_other(q)
+    forward(pieces - 1)
+    finish_other(pieces - 1)
+    for copy in stores:
+        copy.wait()
     drain_all(request_send, request_recv, request_sems)
     drain_all(want_send, fetched, fetch_sems)
     each(n_ent - 1, lambda step: slot_copy(step).wait_send())
@@ -428,13 +483,18 @@
             copy.wait_send()
 
 
-def finish(a_ref, b_ref, rel_ref, entity_ref, relation_ref):
-    entity_ref[...] = a_ref[...].astype(F32) + b_ref[...].astype(F32)
-    block = relation_ref.shape[1]
-    for k in range(relation_ref.shape[0] // LANES):
-        relation_ref[k * LANES : (k + 1) * LANES] = jnp.transpose(
-            rel_ref[k * block : (k + 1) * block].astype(F32)
-        )
+def finish(entity_ref, relation_ref, entity_out, relation_out, sems):
+    copies = []
+    count = sems.shape[1]
+    for k, (src, dst) in enumerate(((relation_ref, relation_out), (entity_ref, entity_out))):
+        rows = src.shape[0] // count
+        for c in range(count):
+            at = pl.ds(c * rows, rows)
+            copies.append(pltpu.make_async_copy(src.at[at], dst.at[at], sems.at[k, c]))
+    for copy in copies:
+        copy.start()
+    for copy in copies:
+        copy.wait()
 
 
 def local(
@@ -455,8 +515,9 @@
     edges = edge_heads.shape[0]
     negs = negative_rows.shape[0]
     r_count, block_count, block, _ = relation_blocks.shape
-    chunk = 256
-    pieces = entities // 2 // chunk
+    chunk = min(512, edges)
+    piece = 128
+    pieces = entities // 2 // piece
     stacked = r_count * width
     flat_rows = stacked * block // LANES
     per_owner = flat_rows // n_ent
@@ -464,13 +525,25 @@
     terms = edges + negs + slot_total
     vmem = pltpu.VMEM
     dma = pltpu.SemaphoreType.DMA
-    spec = pl.BlockSpec(memory_space=pltpu.VMEM)
+    spec = pl.BlockSpec(memory_space=pl.ANY)
     out_shape = (
-        jax.ShapeDtypeStruct((2, pieces, chunk, width), BF16),
-        jax.ShapeDtypeStruct((2, pieces, chunk, width), BF16),
-        jax.ShapeDtypeStruct((n_ent, per_owner, LANES), wire),
+        jax.ShapeDtypeStruct((2, pieces, piece, width), F32),
+        jax.ShapeDtypeStruct((stacked, block), F32),
     )
     scratch = [
+        pltpu.SMEM((1,), jnp.int32),
+        vmem((entities, width), BF16),
+        vmem(request_rows.shape, jnp.int32),
+        vmem((edges // LANES, LANES), jnp.int32),
+        vmem((edges // LANES, LANES), jnp.int32),
+        vmem((edges // LANES, LANES), jnp.int32),
+        vmem((negs // LANES, LANES), jnp.int32),
+        vmem((stacked, block), BF16),
+        vmem((2, pieces, piece, width), BF16),
+        vmem((2, pieces, piece, width), BF16),
+        vmem((n_ent, per_owner, LANES), wire),
+        vmem((2, pieces, piece, width), F32),
+        vmem((stacked, block), F32),
         vmem((n_ent, LANES), jnp.int32),
         vmem((n_ent, 8, LANES), jnp.int32),
         vmem((n_ent, 8, LANES), jnp.int32),
@@ -492,8 +565,8 @@
         vmem((edges, width), BF16),
         vmem((edges, width), BF16),
         vmem((width, edges), BF16),
-        vmem((pieces, chunk, width), BF16),
-        vmem((pieces, chunk, width), BF16),
+        vmem((pieces, piece, width), BF16),
+        vmem((pieces, piece, width), BF16),
         vmem((n_ent, per_owner, LANES), wire),
         vmem((n_ent, per_owner, LANES), wire),
         vmem((per_owner, LANES), wire),
@@ -506,15 +579,18 @@
         dma((2, pieces)),
         dma((2, n_ent)),
         dma((2, n_ent)),
+        dma((8,)),
+        dma((2, pieces)),
+        dma((4,)),
     ]
-    sum_a, sum_b, rel_flat = pl.pallas_call(
+    entity_sum, relation_sum = pl.pallas_call(
         functools.partial(kernel, (n_ent, n_rel)),
         out_shape=out_shape,
-        in_specs=[pl.BlockSpec(memory_space=pltpu.SMEM)] + [spec] * 7,
-        out_specs=(spec,) * 3,
+        in_specs=[spec] * 8,
+        out_specs=(spec,) * 2,
         scratch_shapes=scratch,
         compiler_params=pltpu.CompilerParams(
-            collective_id=0, has_side_effects=True, vmem_limit_bytes=36 * 1024 * 1024
+            collective_id=0, has_side_effects=True, vmem_limit_bytes=56 * 1024 * 1024
         ),
     )(
         edge_counts,
@@ -526,23 +602,17 @@
         negative_rows.reshape(negs // LANES, LANES),
         relation_blocks.reshape(stacked, block),
     )
-    steps = 4
-    tiles = stacked // LANES // steps
-    e_spec = pl.BlockSpec((entities // steps, width), lambda i: (i, 0))
     entity_grad, relation_grad = pl.pallas_call(
         finish,
-        grid=(steps,),
         out_shape=(
             jax.ShapeDtypeStruct((entities, width), F32),
             jax.ShapeDtypeStruct((stacked, block), F32),
         ),
-        in_specs=[e_spec, e_spec, pl.BlockSpec((tiles * block, LANES), lambda i: (i, 0))],
-        out_specs=(e_spec, pl.BlockSpec((tiles * LANES, block), lambda i: (i, 0))),
-    )(
-        sum_a.reshape(entities, width),
-        sum_b.reshape(entities, width),
-        rel_flat.reshape(flat_rows, LANES),
-    )
+        in_specs=[spec] * 2,
+        out_specs=(spec,) * 2,
+        scratch_shapes=[dma((2, 8))],
+        compiler_params=pltpu.CompilerParams(vmem_limit_bytes=56 * 1024 * 1024),
+    )(entity_sum.reshape(entities, width), relation_sum)
     return entity_grad, relation_grad.reshape(relation_blocks.shape)
 
 

time: 45.6 us -> 99.1 us (2.17)
  Pallas kernels: 37.6 us -> 97.6 us
  local copies, waits for them, and re-layouts: 6.34 us -> 0 us
    pallas_call x1, Pallas kernels: 3.62 us -> 64.8 us  [local(): pl.pallas_call(finish, out_shape=(jax.ShapeDtypeStruct((entities, width),...]
    unnamed x20 -> x0, local copies, waits for them, and re-layouts: 6.34 us -> none
    pallas_call x1, Pallas kernels: 34 us -> 32.8 us  [local(): pl.pallas_call(functools.partial(kernel, (n_ent, n_rel)), out_shape=out_s...]
where the time goes in v3:
time: 99.1 us; the launch traced here: 98.9 us
  Pallas kernels  97.6 us (98%)
  between operations  1.29 us (1%)
    pallas_call x1, Pallas kernels, local(): pl.pallas_call(finish, out_shape=(jax.ShapeDtypeStruct((entities, width),...  64.8 us
    pallas_call x1, Pallas kernels, local(): pl.pallas_call(functools.partial(kernel, (n_ent, n_rel)), out_shape=out_s...  32.8 us

profile of v3, /device:TPU:0, one launch (start us, length us, event | category | flops | bytes accessed | tf_op | source)
XLA Modules:
  0.0 98.9 jit_solution(3797245205026028546)
XLA Ops:
  1.3 32.8 %shard_map.95 = (f32[2,4,128,256]{3,2,1,0:T(8,128)}, f32[2048,32]{1,0:T(8,128)}) custom-call(s32[1]{0:T(128)S(6)} %copy.10.counts_hbm, bf16[1024,256]{1,0:T(8,128)(2,1)} %entity_hbm.1, s32[1,8,32]{2,1,0:T(8,128)} %request_hbm.1, s32[8,128]{1,0:T(8,128)} %bitcast.9, s32[8,128]{1,0:T(8,128)} %bitcast.10, s32[8,128]{1,0:T(8,128)} %bitcast.11, ...), custom_call_target="tpu_custom_call" | custom-call | tf_op jit(solution)/shard_map/pallas_call | solution.py:586
  34.1 64.8 %shard_map.96 = (f32[1024,256]{1,0:T(8,128)}, f32[2048,32]{1,0:T(8,128)}) custom-call(f32[1024,256]{1,0:T(8,128)} %bitcast.7, f32[2048,32]{1,0:T(8,128)} %get-tuple-element.7.relation_ref), custom_call_target="tpu_custom_call" | custom-call | tf_op jit(solution)/shard_map/pallas_call | solution.py:605

commit v4 on v3

--- a/solution.py
+++ b/solution.py
@@ -69,7 +69,6 @@
     sum_b_ref,
     rel_out_ref,
     entity_stage,
-    relation_stage,
     request_wide,
     request_send,
     request_recv,
@@ -351,22 +350,37 @@
     grad_proj_t[...] = jnp.transpose(grad_proj[...])
     block_of_lane = iota((block, width), 1) // block
     step_rows = min(block, per_owner)
-    for r in range(r_count):
-        outer = nn(grad_proj_t[...], masked_heads[:, r * width : (r + 1) * width])
-        small = jnp.zeros((block, width), F32)
-        for n in range(width // block):
-            small = small + jnp.where(
-                block_of_lane == n, outer[n * block : (n + 1) * block], 0.0
-            )
-        for c in range(width // LANES):
-            for t in range(block // step_rows):
-                flat = (r * (width // LANES) + c) * block + t * step_rows
-                owner, at = flat // per_owner, flat % per_owner
-                rel_send[owner, at : at + step_rows] = small[
-                    t * step_rows : (t + 1) * step_rows, c * LANES : (c + 1) * LANES
-                ].astype(wire)
-    start_all(rel_send, rel_recv, rs_sems)
-    rel_recv[me] = rel_send[me]
+    owners_per_r = n_ent // r_count
+
+    def relation_terms(first, last):
+        for r in range(first, last):
+            outer = nn(grad_proj_t[...], masked_heads[:, r * width : (r + 1) * width])
+            small = jnp.zeros((block, width), F32)
+            for n in range(width // block):
+                small = small + jnp.where(
+                    block_of_lane == n, outer[n * block : (n + 1) * block], 0.0
+                )
+            for c in range(width // LANES):
+                for t in range(block // step_rows):
+                    flat = (r * (width // LANES) + c) * block + t * step_rows
+                    owner, at = flat // per_owner, flat % per_owner
+                    rel_send[owner, at : at + step_rows] = small[
+                        t * step_rows : (t + 1) * step_rows, c * LANES : (c + 1) * LANES
+                    ].astype(wire)
+            for owner in range(r * owners_per_r, (r + 1) * owners_per_r):
+
+                @pl.when(owner != me)
+                def _():
+                    pltpu.make_async_remote_copy(
+                        src_ref=rel_send.at[owner],
+                        dst_ref=rel_recv.at[me],
+                        send_sem=rs_sems.at[0, owner],
+                        recv_sem=rs_sems.at[1, me],
+                        device_id=(owner, rel),
+                        device_id_type=MESH,
+                    ).start()
+
+    relation_terms(0, r_count // 2)
 
     for i in range(chunks):
         rows = slice(i * chunk, (i + 1) * chunk)
@@ -417,6 +431,8 @@
         copy.start()
         return copy
 
+    relation_terms(r_count // 2, r_count)
+    rel_recv[me] = rel_send[me]
     wait_all(rel_recv, rs_sems)
     total = rel_recv[0].astype(F32)
     for p in range(1, n_ent):
@@ -452,21 +468,9 @@
     for q in range(pieces - 1):
         forward(q)
     wait_all(rel_out_ref, ag_sems)
-    for k in range(relation_stage.shape[0] // LANES):
-        parts = []
-        for t in range(block // step_rows):
-            owner, at = divmod(k * block + t * step_rows, per_owner)
-            parts.append(rel_out_ref[owner, at : at + step_rows].astype(F32))
-        tile = parts[0] if len(parts) == 1 else jnp.concatenate(parts, axis=0)
-        relation_stage[k * LANES : (k + 1) * LANES] = jnp.transpose(tile)
-    store_rows = relation_stage.shape[0] // relation_sems.shape[0]
-    for k in range(relation_sems.shape[0]):
-        rows = pl.ds(k * store_rows, store_rows)
-        copy = pltpu.make_async_copy(
-            relation_stage.at[rows], relation_out.at[rows], relation_sems.at[k]
-        )
-        copy.start()
-        stores.append(copy)
+    copy = pltpu.make_async_copy(rel_out_ref, relation_out, relation_sems.at[0])
+    copy.start()
+    stores.append(copy)
     for q in range(pieces - 1):
         finish_other(q)
     forward(pieces - 1)
@@ -483,18 +487,38 @@
             copy.wait_send()
 
 
-def finish(entity_ref, relation_ref, entity_out, relation_out, sems):
-    copies = []
-    count = sems.shape[1]
-    for k, (src, dst) in enumerate(((relation_ref, relation_out), (entity_ref, entity_out))):
-        rows = src.shape[0] // count
-        for c in range(count):
-            at = pl.ds(c * rows, rows)
-            copies.append(pltpu.make_async_copy(src.at[at], dst.at[at], sems.at[k, c]))
-    for copy in copies:
-        copy.start()
-    for copy in copies:
-        copy.wait()
+def finish(
+    entity_ref, relation_ref, entity_out, relation_out, rel_in, rel_stage, stage, in_sems, out_sems
+):
+    count = out_sems.shape[1]
+    rows = stage.shape[0] // count
+    tall = rel_stage.shape[0] // count
+    block = rel_stage.shape[1]
+    rel_load = pltpu.make_async_copy(relation_ref, rel_in, in_sems.at[count])
+    rel_load.start()
+    loads, stores = [], []
+    for c in range(count):
+        at = pl.ds(c * rows, rows)
+        loads.append(pltpu.make_async_copy(entity_ref.at[at], stage.at[at], in_sems.at[c]))
+        loads[c].start()
+    rel_load.wait()
+    for c in range(count):
+        for k in range(c * tall // LANES, (c + 1) * tall // LANES):
+            rel_stage[k * LANES : (k + 1) * LANES] = jnp.transpose(
+                rel_in[k * block : (k + 1) * block].astype(F32)
+            )
+        at = pl.ds(c * tall, tall)
+        stores.append(
+            pltpu.make_async_copy(rel_stage.at[at], relation_out.at[at], out_sems.at[1, c])
+        )
+        stores[-1].start()
+    for c in range(count):
+        loads[c].wait()
+        at = pl.ds(c * rows, rows)
+        stores.append(pltpu.make_async_copy(stage.at[at], entity_out.at[at], out_sems.at[0, c]))
+        stores[-1].start()
+    for store in stores:
+        store.wait()
 
 
 def local(
@@ -528,7 +552,7 @@
     spec = pl.BlockSpec(memory_space=pl.ANY)
     out_shape = (
         jax.ShapeDtypeStruct((2, pieces, piece, width), F32),
-        jax.ShapeDtypeStruct((stacked, block), F32),
+        jax.ShapeDtypeStruct((n_ent, per_owner, LANES), wire),
     )
     scratch = [
         pltpu.SMEM((1,), jnp.int32),
@@ -543,7 +567,6 @@
         vmem((2, pieces, piece, width), BF16),
         vmem((n_ent, per_owner, LANES), wire),
         vmem((2, pieces, piece, width), F32),
-        vmem((stacked, block), F32),
         vmem((n_ent, LANES), jnp.int32),
         vmem((n_ent, 8, LANES), jnp.int32),
         vmem((n_ent, 8, LANES), jnp.int32),
@@ -581,7 +604,7 @@
         dma((2, n_ent)),
         dma((8,)),
         dma((2, pieces)),
-        dma((4,)),
+        dma((1,)),
     ]
     entity_sum, relation_sum = pl.pallas_call(
         functools.partial(kernel, (n_ent, n_rel)),
@@ -610,9 +633,15 @@
         ),
         in_specs=[spec] * 2,
         out_specs=(spec,) * 2,
-        scratch_shapes=[dma((2, 8))],
+        scratch_shapes=[
+            vmem((flat_rows, LANES), wire),
+            vmem((stacked, block), F32),
+            vmem((entities, width), F32),
+            dma((9,)),
+            dma((2, 8)),
+        ],
         compiler_params=pltpu.CompilerParams(vmem_limit_bytes=56 * 1024 * 1024),
-    )(entity_sum.reshape(entities, width), relation_sum)
+    )(entity_sum.reshape(entities, width), relation_sum.reshape(flat_rows, LANES))
     return entity_grad, relation_grad.reshape(relation_blocks.shape)
 
 

time: 99.1 us -> 41.2 us (0.42)
  the two profiles are of different devices: /device:TPU:0 before, /device:TPU:1 now
where the time goes in v4:
time: 41.2 us; the launch traced here: 41 us
  Pallas kernels  39.7 us (96%)
  between operations  1.29 us (3%)
    pallas_call x1, Pallas kernels, local(): pl.pallas_call(functools.partial(kernel, (n_ent, n_rel)), out_shape=out_s...  37.2 us
    pallas_call x1, Pallas kernels, local(): pl.pallas_call(finish, out_shape=(jax.ShapeDtypeStruct((entities, width),...  2.53 us

profile of v4, /device:TPU:1, one launch (start us, length us, event | category | flops | bytes accessed | tf_op | source)
XLA Modules:
  0.0 41.0 jit_solution(18161283314404810759)
XLA Ops:
  1.3 37.2 %shard_map.95 = (f32[2,4,128,256]{3,2,1,0:T(8,128)}, bf16[8,64,128]{2,1,0:T(8,128)(2,1)}) custom-call(s32[1]{0:T(128)S(6)} %copy.10.counts_hbm, bf16[1024,256]{1,0:T(8,128)(2,1)} %entity_hbm.1, s32[1,8,32]{2,1,0:T(8,128)} %request_hbm.1, s32[8,128]{1,0:T(8,128)} %bitcast.11, s32[8,128]{1,0:T(8,128)} %bitcast.12, s32[8,128]{1,0:T(8,128)} %bitcast.13, ...), custom_call_target="tpu_custom_call" | custom-call | tf_op jit(solution)/shard_map/pallas_call | solution.py:609
  38.5 2.5 %shard_map.96 = (f32[1024,256]{1,0:T(8,128)}, f32[2048,32]{1,0:T(8,128)}) custom-call(f32[1024,256]{1,0:T(8,128)} %bitcast.8, bf16[512,128]{1,0:T(8,128)(2,1)} %bitcast.10), custom_call_target="tpu_custom_call" | custom-call | tf_op jit(solution)/shard_map/pallas_call | solution.py:628

commit v5 on v4

--- a/solution.py
+++ b/solution.py
@@ -92,6 +92,7 @@
     grad_proj_t,
     part_send,
     part_recv,
+    own_half,
     rel_send,
     rel_recv,
     rel_own,
@@ -350,8 +351,6 @@
     grad_proj_t[...] = jnp.transpose(grad_proj[...])
     block_of_lane = iota((block, width), 1) // block
     step_rows = min(block, per_owner)
-    owners_per_r = n_ent // r_count
-
     def relation_terms(first, last):
         for r in range(first, last):
             outer = nn(grad_proj_t[...], masked_heads[:, r * width : (r + 1) * width])
@@ -367,20 +366,10 @@
                     rel_send[owner, at : at + step_rows] = small[
                         t * step_rows : (t + 1) * step_rows, c * LANES : (c + 1) * LANES
                     ].astype(wire)
-            for owner in range(r * owners_per_r, (r + 1) * owners_per_r):
-
-                @pl.when(owner != me)
-                def _():
-                    pltpu.make_async_remote_copy(
-                        src_ref=rel_send.at[owner],
-                        dst_ref=rel_recv.at[me],
-                        send_sem=rs_sems.at[0, owner],
-                        recv_sem=rs_sems.at[1, me],
-                        device_id=(owner, rel),
-                        device_id_type=MESH,
-                    ).start()
-
-    relation_terms(0, r_count // 2)
+
+    relation_terms(0, r_count)
+    start_all(rel_send, rel_recv, rs_sems)
+    rel_recv[me] = rel_send[me]
 
     for i in range(chunks):
         rows = slice(i * chunk, (i + 1) * chunk)
@@ -414,25 +403,7 @@
             part_copies.append(near_copy(part_send.at[q], part_recv.at[q], part_sems, q, near))
     for g in range(pieces // pair):
         at = pl.multiple_of(core * half + g * pair * piece, pair * piece)
-        own = nn(scatter_hot[pl.ds(at, pair * piece)], grads[...])
-        for q in range(g * pair, (g + 1) * pair):
-            low = (q - g * pair) * piece
-            part_copies[q].wait_recv()
-            sum_a_ref[core, q] = (own[low : low + piece] + part_recv[q].astype(F32)).astype(BF16)
-            mine = sum_a_ref.at[core, q]
-            cross_copies.append(near_copy(mine, sum_b_ref.at[core, q], cross_sems, q, cross))
-            near_copies.append(near_copy(mine, mine, near_sems, q, near))
-
-    def write_entity(which, q):
-        entity_stage[which, q] = sum_a_ref[which, q].astype(F32) + sum_b_ref[which, q].astype(F32)
-        copy = pltpu.make_async_copy(
-            entity_stage.at[which, q], entity_out.at[which, q], entity_sems.at[which, q]
-        )
-        copy.start()
-        return copy
-
-    relation_terms(r_count // 2, r_count)
-    rel_recv[me] = rel_send[me]
+        own_half[g] = nn(scatter_hot[pl.ds(at, pair * piece)], grads[...])
     wait_all(rel_recv, rs_sems)
     total = rel_recv[0].astype(F32)
     for p in range(1, n_ent):
@@ -452,6 +423,24 @@
         )
 
     each(n_ent - 1, lambda step: gather_copy(step).start())
+    for g in range(pieces // pair):
+        own = own_half[g]
+        for q in range(g * pair, (g + 1) * pair):
+            low = (q - g * pair) * piece
+            part_copies[q].wait_recv()
+            sum_a_ref[core, q] = (own[low : low + piece] + part_recv[q].astype(F32)).astype(BF16)
+            mine = sum_a_ref.at[core, q]
+            cross_copies.append(near_copy(mine, sum_b_ref.at[core, q], cross_sems, q, cross))
+            near_copies.append(near_copy(mine, mine, near_sems, q, near))
+
+    def write_entity(which, q):
+        entity_stage[which, q] = sum_a_ref[which, q].astype(F32) + sum_b_ref[which, q].astype(F32)
+        copy = pltpu.make_async_copy(
+            entity_stage.at[which, q], entity_out.at[which, q], entity_sems.at[which, q]
+        )
+        copy.start()
+        return copy
+
     stores = []
 
     def forward(q):
@@ -549,7 +538,7 @@
     terms = edges + negs + slot_total
     vmem = pltpu.VMEM
     dma = pltpu.SemaphoreType.DMA
-    spec = pl.BlockSpec(memory_space=pl.ANY)
+    spec = pl.BlockSpec(memory_space=pltpu.HBM)
     out_shape = (
         jax.ShapeDtypeStruct((2, pieces, piece, width), F32),
         jax.ShapeDtypeStruct((n_ent, per_owner, LANES), wire),
@@ -590,6 +579,7 @@
         vmem((width, edges), BF16),
         vmem((pieces, piece, width), BF16),
         vmem((pieces, piece, width), BF16),
+        vmem((pieces // 2, 2 * piece, width), F32),
         vmem((n_ent, per_owner, LANES), wire),
         vmem((n_ent, per_owner, LANES), wire),
         vmem((per_owner, LANES), wire),

time: 41.2 us -> 37 us (0.90)
  the two profiles are of different devices: /device:TPU:1 before, /device:TPU:0 now
where the time goes in v5:
time: 37 us; the launch traced here: 36.8 us
  Pallas kernels  35.5 us (96%)
  between operations  1.29 us (3%)
    pallas_call x1, Pallas kernels, local(): pl.pallas_call(functools.partial(kernel, (n_ent, n_rel)), out_shape=out_s...  33 us
    pallas_call x1, Pallas kernels, local(): pl.pallas_call(finish, out_shape=(jax.ShapeDtypeStruct((entities, width),...  2.53 us

profile of v5, /device:TPU:0, one launch (start us, length us, event | category | flops | bytes accessed | tf_op | source)
XLA Modules:
  0.0 36.8 jit_solution(17627764293871313849)
XLA Ops:
  1.3 33.0 %shard_map.95 = (f32[2,4,128,256]{3,2,1,0:T(8,128)}, bf16[8,64,128]{2,1,0:T(8,128)(2,1)}) custom-call(s32[1]{0:T(128)S(6)} %copy.10.counts_hbm, bf16[1024,256]{1,0:T(8,128)(2,1)} %entity_hbm.1, s32[1,8,32]{2,1,0:T(8,128)} %request_hbm.1, s32[8,128]{1,0:T(8,128)} %bitcast.11, s32[8,128]{1,0:T(8,128)} %bitcast.12, s32[8,128]{1,0:T(8,128)} %bitcast.13, ...), custom_call_target="tpu_custom_call" | custom-call | tf_op jit(solution)/shard_map/pallas_call | solution.py:599
  34.3 2.5 %shard_map.96 = (f32[1024,256]{1,0:T(8,128)}, f32[2048,32]{1,0:T(8,128)}) custom-call(f32[1024,256]{1,0:T(8,128)} %bitcast.8, bf16[512,128]{1,0:T(8,128)(2,1)} %bitcast.10), custom_call_target="tpu_custom_call" | custom-call | tf_op jit(solution)/shard_map/pallas_call | solution.py:618

commit v6 on v5

--- a/solution.py
+++ b/solution.py
@@ -121,7 +121,7 @@
     negs = negs_ref.shape[0] * LANES
     block = blocks_ref.shape[1]
     r_count = blocks_ref.shape[0] // width
-    chunk = masked_grads.shape[0]
+    chunk = hot_rows.shape[0]
     chunks = edges // chunk
     piece = sum_a_ref.shape[2]
     per = LANES // slots
@@ -231,8 +231,13 @@
     for r in range(r_count):
         rows = slice(r * width, (r + 1) * width)
         one = blocks_ref[rows]
-        operators[rows] = jnp.where(diagonal, nn(one, spread), 0.0).astype(BF16)
-        operators_t[rows] = jnp.where(diagonal, nt(spread_t, one), 0.0).astype(BF16)
+        plain = jnp.where(diagonal, nn(one, spread), 0.0).astype(BF16)
+        turned = jnp.where(diagonal, nt(spread_t, one), 0.0).astype(BF16)
+        for c in range(width // LANES):
+            part = slice(c * LANES, (c + 1) * LANES)
+            at = (c * r_count + r) * LANES
+            operators[at : at + LANES] = plain[part]
+            operators_t[at : at + LANES] = turned[part]
 
     def rel_masks(rows):
         ids = (codes[rows] >> head_bits) & (r_count - 1)
@@ -241,7 +246,7 @@
     def mask_by_rel(source, masks, target, rows):
         for r in range(r_count):
             for c in range(width // LANES):
-                at = r * width + c * LANES
+                at = (c * r_count + r) * LANES
                 target[rows, at : at + LANES] = source[:, c * LANES : (c + 1) * LANES] * masks[r]
 
     wide_lane = iota((chunk, LANES), 1)
@@ -349,37 +354,35 @@
     wire = rel_send.dtype
     per_owner = rel_send.shape[1]
     grad_proj_t[...] = jnp.transpose(grad_proj[...])
-    block_of_lane = iota((block, width), 1) // block
     step_rows = min(block, per_owner)
-    def relation_terms(first, last):
-        for r in range(first, last):
-            outer = nn(grad_proj_t[...], masked_heads[:, r * width : (r + 1) * width])
-            small = jnp.zeros((block, width), F32)
-            for n in range(width // block):
-                small = small + jnp.where(
-                    block_of_lane == n, outer[n * block : (n + 1) * block], 0.0
-                )
-            for c in range(width // LANES):
-                for t in range(block // step_rows):
-                    flat = (r * (width // LANES) + c) * block + t * step_rows
-                    owner, at = flat // per_owner, flat % per_owner
-                    rel_send[owner, at : at + step_rows] = small[
-                        t * step_rows : (t + 1) * step_rows, c * LANES : (c + 1) * LANES
-                    ].astype(wire)
-
-    relation_terms(0, r_count)
+    span = r_count * LANES
+    block_of_lane = iota((block, span), 1) // block % (LANES // block)
+    for c in range(width // LANES):
+        outer = nn(
+            grad_proj_t[c * LANES : (c + 1) * LANES], masked_heads[:, c * span : (c + 1) * span]
+        )
+        small = jnp.zeros((block, span), F32)
+        for n in range(LANES // block):
+            small = jnp.where(block_of_lane == n, outer[n * block : (n + 1) * block], small)
+        for r in range(r_count):
+            for t in range(block // step_rows):
+                flat = (r * (width // LANES) + c) * block + t * step_rows
+                owner, at = flat // per_owner, flat % per_owner
+                rel_send[owner, at : at + step_rows] = small[
+                    t * step_rows : (t + 1) * step_rows, r * LANES : (r + 1) * LANES
+                ].astype(wire)
     start_all(rel_send, rel_recv, rs_sems)
     rel_recv[me] = rel_send[me]
 
     for i in range(chunks):
         rows = slice(i * chunk, (i + 1) * chunk)
-        mask_by_rel(grad_proj[rows], rel_masks(rows), masked_grads, slice(0, chunk))
-        grads[rows] = nn(masked_grads[...], operators_t[...]).astype(BF16)
+        mask_by_rel(grad_proj[rows], rel_masks(rows), masked_grads, rows)
+    grads[:edges] = nn(masked_grads[...], operators_t[...]).astype(BF16)
 
     each(n_ent - 1, lambda step: slot_arrival(step).wait_recv())
 
     pieces = half // piece
-    pair = 2
+    pair = pieces
     part_copies, cross_copies, near_copies, far_copies = [], [], [], []
 
     def near_copy(src, dst, sems, q, target):
@@ -570,7 +573,7 @@
         vmem((stacked, width), BF16),
         vmem((stacked, width), BF16),
         vmem((edges, stacked), BF16),
-        vmem((chunk, stacked), BF16),
+        vmem((edges, stacked), BF16),
         vmem((edges, width), BF16),
         vmem((edges, negs), BF16),
         vmem((negs, width), BF16),
@@ -579,7 +582,7 @@
         vmem((width, edges), BF16),
         vmem((pieces, piece, width), BF16),
         vmem((pieces, piece, width), BF16),
-        vmem((pieces // 2, 2 * piece, width), F32),
+        vmem((1, pieces * piece, width), F32),
         vmem((n_ent, per_owner, LANES), wire),
         vmem((n_ent, per_owner, LANES), wire),
         vmem((per_owner, LANES), wire),

time: 37 us -> 37.4 us (1.011)
  Pallas kernels: 35.5 us -> 35.9 us
    pallas_call x1, Pallas kernels: 33 us -> 33.4 us  [local(): pl.pallas_call(functools.partial(kernel, (n_ent, n_rel)), out_shape=out_s...]
where the time goes in v6:
time: 37.4 us; the launch traced here: 37.2 us
  Pallas kernels  35.9 us (96%)
  between operations  1.29 us (3%)
    pallas_call x1, Pallas kernels, local(): pl.pallas_call(functools.partial(kernel, (n_ent, n_rel)), out_shape=out_s...  33.4 us
    pallas_call x1, Pallas kernels, local(): pl.pallas_call(finish, out_shape=(jax.ShapeDtypeStruct((entities, width),...  2.53 us

profile of v6, /device:TPU:0, one launch (start us, length us, event | category | flops | bytes accessed | tf_op | source)
XLA Modules:
  0.0 37.2 jit_solution(4285722971720080982)
XLA Ops:
  1.3 33.4 %shard_map.95 = (f32[2,4,128,256]{3,2,1,0:T(8,128)}, bf16[8,64,128]{2,1,0:T(8,128)(2,1)}) custom-call(s32[1]{0:T(128)S(6)} %copy.10.counts_hbm, bf16[1024,256]{1,0:T(8,128)(2,1)} %entity_hbm.1, s32[1,8,32]{2,1,0:T(8,128)} %request_hbm.1, s32[8,128]{1,0:T(8,128)} %bitcast.11, s32[8,128]{1,0:T(8,128)} %bitcast.12, s32[8,128]{1,0:T(8,128)} %bitcast.13, ...), custom_call_target="tpu_custom_call" | custom-call | tf_op jit(solution)/shard_map/pallas_call | solution.py:602
  34.7 2.5 %shard_map.96 = (f32[1024,256]{1,0:T(8,128)}, f32[2048,32]{1,0:T(8,128)}) custom-call(f32[1024,256]{1,0:T(8,128)} %bitcast.8, bf16[512,128]{1,0:T(8,128)(2,1)} %bitcast.10), custom_call_target="tpu_custom_call" | custom-call | tf_op jit(solution)/shard_map/pallas_call | solution.py:621

commit v7 on v6

--- a/solution.py
+++ b/solution.py
@@ -88,10 +88,12 @@
     neg_weight,
     neg_rows,
     weighted,
+    pos_tail,
     grad_proj,
     grad_proj_t,
     part_send,
     part_recv,
+    part_half,
     own_half,
     rel_send,
     rel_recv,
@@ -317,7 +319,7 @@
         live = iota((chunk, 1), 0) + i * chunk < live_count
         pos_weight = jnp.where(live, -jax.nn.sigmoid(-positive), 0.0)
         weighted[rows] = (pos_weight * proj).astype(BF16)
-        grad_proj[rows] = (pos_weight * tail + nn(neg_weight[rows], neg_rows[...])).astype(BF16)
+        pos_tail[rows] = pos_weight * tail
     per_step = min(n_ent, 8)
     for g in range(n_ent // per_step):
         rows = slice(g * per_step * slots, (g + 1) * per_step * slots)
@@ -350,6 +352,10 @@
 
     each(n_ent - 1, lambda step: slot_copy(step).start())
     grads[pl.ds(pl.multiple_of(slot_at + me * slots, slots), slots)] = slot_send[me]
+
+    for i in range(chunks):
+        rows = slice(i * chunk, (i + 1) * chunk)
+        grad_proj[rows] = (pos_tail[rows] + nn(neg_weight[rows], neg_rows[...])).astype(BF16)
 
     wire = rel_send.dtype
     per_owner = rel_send.shape[1]
@@ -379,8 +385,6 @@
         mask_by_rel(grad_proj[rows], rel_masks(rows), masked_grads, rows)
     grads[:edges] = nn(masked_grads[...], operators_t[...]).astype(BF16)
 
-    each(n_ent - 1, lambda step: slot_arrival(step).wait_recv())
-
     pieces = half // piece
     pair = pieces
     part_copies, cross_copies, near_copies, far_copies = [], [], [], []
@@ -397,16 +401,39 @@
         copy.start()
         return copy
 
+    def scatter(which, g, terms):
+        at = pl.multiple_of(which * half + g * pair * piece, pair * piece)
+        return nn(scatter_hot[pl.ds(at, pair * piece), terms], grads[terms])
+
+    early, late = slice(0, slot_at), slice(slot_at, slot_at + slot_total)
     for g in range(pieces // pair):
-        at = pl.multiple_of((1 - core) * half + g * pair * piece, pair * piece)
-        part = nn(scatter_hot[pl.ds(at, pair * piece)], grads[...]).astype(BF16)
+        part_half[g] = scatter(1 - core, g, early)
+        own_half[g] = scatter(core, g, early)
+    each(n_ent - 1, lambda step: slot_arrival(step).wait_recv())
+    for g in range(pieces // pair):
+        part = (part_half[g] + scatter(1 - core, g, late)).astype(BF16)
         for q in range(g * pair, (g + 1) * pair):
             low = (q - g * pair) * piece
             part_send[q] = part[low : low + piece]
             part_copies.append(near_copy(part_send.at[q], part_recv.at[q], part_sems, q, near))
     for g in range(pieces // pair):
-        at = pl.multiple_of(core * half + g * pair * piece, pair * piece)
-        own_half[g] = nn(scatter_hot[pl.ds(at, pair * piece)], grads[...])
+        own = own_half[g] + scatter(core, g, late)
+        for q in range(g * pair, (g + 1) * pair):
+            low = (q - g * pair) * piece
+            part_copies[q].wait_recv()
+            sum_a_ref[core, q] = (own[low : low + piece] + part_recv[q].astype(F32)).astype(BF16)
+            mine = sum_a_ref.at[core, q]
+            cross_copies.append(near_copy(mine, sum_b_ref.at[core, q], cross_sems, q, cross))
+            near_copies.append(near_copy(mine, mine, near_sems, q, near))
+
+    def write_entity(which, q):
+        entity_stage[which, q] = sum_a_ref[which, q].astype(F32) + sum_b_ref[which, q].astype(F32)
+        copy = pltpu.make_async_copy(
+            entity_stage.at[which, q], entity_out.at[which, q], entity_sems.at[which, q]
+        )
+        copy.start()
+        return copy
+
     wait_all(rel_recv, rs_sems)
     total = rel_recv[0].astype(F32)
     for p in range(1, n_ent):
@@ -426,24 +453,6 @@
         )
 
     each(n_ent - 1, lambda step: gather_copy(step).start())
-    for g in range(pieces // pair):
-        own = own_half[g]
-        for q in range(g * pair, (g + 1) * pair):
-            low = (q - g * pair) * piece
-            part_copies[q].wait_recv()
-            sum_a_ref[core, q] = (own[low : low + piece] + part_recv[q].astype(F32)).astype(BF16)
-            mine = sum_a_ref.at[core, q]
-            cross_copies.append(near_copy(mine, sum_b_ref.at[core, q], cross_sems, q, cross))
-            near_copies.append(near_copy(mine, mine, near_sems, q, near))
-
-    def write_entity(which, q):
-        entity_stage[which, q] = sum_a_ref[which, q].astype(F32) + sum_b_ref[which, q].astype(F32)
-        copy = pltpu.make_async_copy(
-            entity_stage.at[which, q], entity_out.at[which, q], entity_sems.at[which, q]
-        )
-        copy.start()
-        return copy
-
     stores = []
 
     def forward(q):
@@ -578,10 +587,12 @@
         vmem((edges, negs), BF16),
         vmem((negs, width), BF16),
         vmem((edges, width), BF16),
+        vmem((edges, width), F32),
         vmem((edges, width), BF16),
         vmem((width, edges), BF16),
         vmem((pieces, piece, width), BF16),
         vmem((pieces, piece, width), BF16),
+        vmem((1, pieces * piece, width), F32),
         vmem((1, pieces * piece, width), F32),
         vmem((n_ent, per_owner, LANES), wire),
         vmem((n_ent, per_owner, LANES), wire),

time: 37.4 us -> 36.2 us (0.968)
  Pallas kernels: 35.9 us -> 34.7 us
    pallas_call x1, Pallas kernels: 33.4 us -> 32.1 us  [local(): pl.pallas_call(functools.partial(kernel, (n_ent, n_rel)), out_shape=out_s...]
where the time goes in v7:
time: 36.2 us; the launch traced here: 35.9 us
  Pallas kernels  34.7 us (96%)
  between operations  1.29 us (4%)
    pallas_call x1, Pallas kernels, local(): pl.pallas_call(functools.partial(kernel, (n_ent, n_rel)), out_shape=out_s...  32.1 us
    pallas_call x1, Pallas kernels, local(): pl.pallas_call(finish, out_shape=(jax.ShapeDtypeStruct((entities, width),...  2.53 us

profile of v7, /device:TPU:0, one launch (start us, length us, event | category | flops | bytes accessed | tf_op | source)
XLA Modules:
  0.0 35.9 jit_solution(18219152909929699919)
XLA Ops:
  1.3 32.1 %shard_map.95 = (f32[2,4,128,256]{3,2,1,0:T(8,128)}, bf16[8,64,128]{2,1,0:T(8,128)(2,1)}) custom-call(s32[1]{0:T(128)S(6)} %copy.10.counts_hbm, bf16[1024,256]{1,0:T(8,128)(2,1)} %entity_hbm.1, s32[1,8,32]{2,1,0:T(8,128)} %request_hbm.1, s32[8,128]{1,0:T(8,128)} %bitcast.11, s32[8,128]{1,0:T(8,128)} %bitcast.12, s32[8,128]{1,0:T(8,128)} %bitcast.13, ...), custom_call_target="tpu_custom_call" | custom-call | tf_op jit(solution)/shard_map/pallas_call | solution.py:613
  33.4 2.5 %shard_map.96 = (f32[1024,256]{1,0:T(8,128)}, f32[2048,32]{1,0:T(8,128)}) custom-call(f32[1024,256]{1,0:T(8,128)} %bitcast.8, bf16[512,128]{1,0:T(8,128)(2,1)} %bitcast.10), custom_call_target="tpu_custom_call" | custom-call | tf_op jit(solution)/shard_map/pallas_call | solution.py:632

commit v8 on v7

--- a/solution.py
+++ b/solution.py
@@ -268,7 +268,15 @@
         neg_weight[rows] = weight
         return tn(weight, proj)
 
-    neg_grad = project(0)
+    sub = iota((entities, LANES), 0)
+    for k in range(edges // LANES):
+        scatter_hot[:, k * LANES : (k + 1) * LANES] = hot(sub == heads_ref[k : k + 1])
+    for k in range(negs // LANES):
+        at = neg_at + k * LANES
+        scatter_hot[:, at : at + LANES] = hot(sub == negs_ref[k : k + 1])
+    slot_sub = iota((slot_total, LANES), 0)
+    for k in range(edges // LANES):
+        tail_hot_t[:, k * LANES : (k + 1) * LANES] = hot(slot_sub == tails_ref[k : k + 1])
 
     wait_all(request_recv, request_sems)
     request_rows = []
@@ -288,22 +296,14 @@
     fetched[me] = want_send[me]
     start_all(want_send, fetched, fetch_sems)
 
+    neg_grad = project(0)
     for i in range(1, chunks):
         neg_grad = neg_grad + project(i)
     grads[neg_at : neg_at + negs] = neg_grad.astype(BF16)
 
-    sub = iota((entities, LANES), 0)
-    for k in range(edges // LANES):
-        scatter_hot[:, k * LANES : (k + 1) * LANES] = hot(sub == heads_ref[k : k + 1])
-    for k in range(negs // LANES):
-        at = neg_at + k * LANES
-        scatter_hot[:, at : at + LANES] = hot(sub == negs_ref[k : k + 1])
     for k, row in enumerate(request_rows):
         at = slot_at + k * LANES
         scatter_hot[:, at : at + LANES] = hot(sub == row)
-    slot_sub = iota((slot_total, LANES), 0)
-    for k in range(edges // LANES):
-        tail_hot_t[:, k * LANES : (k + 1) * LANES] = hot(slot_sub == tails_ref[k : k + 1])
 
     wait_all(fetched, fetch_sems)
     table = fetched[...].reshape(slot_total, width)

time: 36.2 us -> 36.2 us (level)
  no operation moved by 1% of the time
where the time goes in v8:
time: 36.2 us; the launch traced here: 36 us
  Pallas kernels  34.7 us (96%)
  between operations  1.29 us (4%)
    pallas_call x1, Pallas kernels, local(): pl.pallas_call(functools.partial(kernel, (n_ent, n_rel)), out_shape=out_s...  32.2 us
    pallas_call x1, Pallas kernels, local(): pl.pallas_call(finish, out_shape=(jax.ShapeDtypeStruct((entities, width),...  2.53 us

profile of v8, /device:TPU:0, one launch (start us, length us, event | category | flops | bytes accessed | tf_op | source)
XLA Modules:
  0.0 36.0 jit_solution(17109599574008881058)
XLA Ops:
  1.3 32.2 %shard_map.95 = (f32[2,4,128,256]{3,2,1,0:T(8,128)}, bf16[8,64,128]{2,1,0:T(8,128)(2,1)}) custom-call(s32[1]{0:T(128)S(6)} %copy.10.counts_hbm, bf16[1024,256]{1,0:T(8,128)(2,1)} %entity_hbm.1, s32[1,8,32]{2,1,0:T(8,128)} %request_hbm.1, s32[8,128]{1,0:T(8,128)} %bitcast.11, s32[8,128]{1,0:T(8,128)} %bitcast.12, s32[8,128]{1,0:T(8,128)} %bitcast.13, ...), custom_call_target="tpu_custom_call" | custom-call | tf_op jit(solution)/shard_map/pallas_call | solution.py:613
  33.4 2.5 %shard_map.96 = (f32[1024,256]{1,0:T(8,128)}, f32[2048,32]{1,0:T(8,128)}) custom-call(f32[1024,256]{1,0:T(8,128)} %bitcast.8, bf16[512,128]{1,0:T(8,128)(2,1)} %bitcast.10), custom_call_target="tpu_custom_call" | custom-call | tf_op jit(solution)/shard_map/pallas_call | solution.py:632
